TPU v7x, 256 devices: a whole 4x4x8 slice. The times are simulated.
256 devices in a mesh: row: 32 (over z_lo, x, core), col: 8 (over y, z_hi).
Axes of the slice: x: 4, y: 4, z: 8 (z_hi: 2, z_lo: 4; z = z_hi * 4 + z_lo), core: 2. Of those that a mesh axis runs over, the one named last changes fastest.
Arguments:
- layer_input: bfloat16 [2048, 16384], P('row', 'col'), may hold values from -6 to 6
- out_grad: bfloat16 [2048, 26624], P('row', 'col'), may hold values from -6 to 6
- up_weight: bfloat16 [16384, 26624], P('row', 'col'), may hold values from -0.046875 to 0.046875
Outputs:
- input_grad: bfloat16 [2048, 16384], P('row', 'col')
- weight_grad: float32 [16384, 26624], P('row', 'col')
All inputs are finite; a program needn't handle non-finite values.
Results may differ from a plain program's by a relative error of at most 0.0012.
Values may be sent and summed in bfloat16 or wider, within the bound.
No kernel may reach another device: no remote copies, remote signals or barrier semaphores. Data moves between devices by JAX's collectives and lax.ppermute only.
A program may use at most 128 MiB of HBM per device.

v0:
```python
import math

import jax
import jax.numpy as jnp
from jax import lax
from jax.sharding import PartitionSpec as P


def local(layer_input, out_grad, up_weight):
    n_row = lax.axis_size("row")
    rows_here = layer_input.shape[0]
    total_rows = rows_here * n_row
    all_features = lax.all_gather(layer_input, "col", axis=1, tiled=True)
    column_slab = lax.all_to_all(all_features, "row", split_axis=1, concat_axis=0, tiled=True)
    grad_all = lax.all_gather(out_grad, "row", axis=0, tiled=True)
    weight_grad = lax.dot_general(
        column_slab, grad_all, (((0,), (0,)), ((), ())), preferred_element_type=jnp.float32
    )
    weight_grad = weight_grad * (1.0 / math.sqrt(total_rows))
    partial_value = lax.dot_general(
        grad_all, up_weight, (((1,), (1,)), ((), ())), preferred_element_type=jnp.float32
    )
    moved = lax.all_to_all(partial_value, "row", split_axis=0, concat_axis=1, tiled=True)
    input_grad = lax.psum_scatter(moved, "col", scatter_dimension=1, tiled=True).astype(
        jnp.bfloat16
    )
    return (input_grad, weight_grad)


def solution(mesh):
    in_specs = (P("row", "col"), P("row", "col"), P("row", "col"))
    out_specs = (P("row", "col"), P("row", "col"))
    return jax.shard_map(local, mesh=mesh, in_specs=in_specs, out_specs=out_specs, check_vma=False)
```

profile of v0, /device:TPU:7, one launch (start us, length us, event | category | flops | bytes accessed | tf_op | source)
XLA Modules:
  0.0 383.1 jit_solution(11272415930034361604)
XLA Ops:
  8.0 0.0 copy-start
  8.0 0.0 all-gather.3.cloned.1.call-start
  8.1 0.7 all-gather.3.cloned.1.call-update
  8.7 89.2 %all-gather.3.cloned.1.call-done = bf16[2048,3328]{1,0:T(8,128)(2,1)} async-done(((bf16[64,3328]{1,0:T(8,128)(2,1)}), bf16[2048,3328]{1,0:T(8,128)(2,1)}) %all-gather.3.cloned.1.call-update) | async-done | bytes 13631504 | tf_op jit(solution)/shard_map/all_gather | solution.py:15
  97.9 0.0 copy-done
  97.9 11.7 %fusion = f32[2048,512]{1,0:T(8,128)} fusion(bf16[2048,3328]{1,0:T(8,128)(2,1)} %all-gather.3.cloned.1.call-done, bf16[512,3328]{1,0:T(8,128)(2,1)S(1)} %copy-done), kind=kOutput, calls=%fused_computation.2 | convolution fusion | flops 6979321856 | bytes 21233664 | tf_op jit(solution)/shard_map/dot_general | solution.py:20
  109.6 7.6 %all-to-all-start = ((f32[32,64,512]{2,1,0:T(8,128)}), f32[32,64,512]{2,1,0:T(8,128)}, u32[]{:S(2)}, u32[]{:S(2)}) async-start(f32[32,64,512]{2,1,0:T(8,128)} %bitcast.17), calls=%async_computation | async-start | bytes 8388608 | tf_op jit(solution)/shard_map/all_to_all | solution.py:23
  117.2 0.0 all-gather.5.cloned.1.call-start
  117.2 0.5 all-gather.5.cloned.1.call-update
  117.7 0.0 reduce-scatter.2.cloned.1.call-start
  117.8 120.4 %all-to-all-done = f32[32,64,512]{2,1,0:T(8,128)} async-done(((f32[32,64,512]{2,1,0:T(8,128)}), f32[32,64,512]{2,1,0:T(8,128)}, u32[]{:S(2)}, u32[]{:S(2)}) %all-to-all-start) | async-done | bytes 4194336 | tf_op jit(solution)/shard_map/all_to_all | solution.py:23
  238.2 4.7 %copy.12 = f32[32,8,8,512]{3,2,0,1:T(8,128)} copy(f32[32,8,8,512]{3,2,1,0:T(8,128)} %bitcast.7) | data formatting | bytes 8388608 | tf_op jit(solution)/shard_map/all_to_all | solution.py:23
  242.9 0.0 reduce-scatter.2.cloned.1.call-update
  242.9 0.0 all-gather.5.cloned.1.call-done
  243.0 1.9 copy.14
  244.8 100.1 %all_to_all.38 = bf16[64,32,512]{2,0,1:T(8,128)(2,1)S(1)} all-to-all(bf16[64,32,512]{2,0,1:T(8,128)(2,1)S(1)} %bitcast.16), channel_id=1, replica_groups=mesh['row'=32,'col'=8] {'row'}, dimensions={1} | all-to-all | bytes 4194304 | tf_op jit(solution)/shard_map/all_to_all | solution.py:14
  344.9 12.8 %convolution_multiply_fusion = f32[512,3328]{1,0:T(8,128)} fusion(bf16[2048,512]{1,0:T(8,128)(2,1)S(1)} %bitcast.19, bf16[2048,3328]{1,0:T(8,128)(2,1)} %all-gather.3.cloned.1.call-done), kind=kOutput, calls=%fused_computation | convolution fusion | flops 6981025792 | bytes 22544384 | tf_op jit(solution)/shard_map/dot_general | solution.py:16
  357.7 16.2 %reduce-scatter.2.cloned.1.call-done = f32[64,2048]{1,0:T(8,128)} async-done(((f32[64,16384]{1,0:T(8,128)}), f32[64,2048]{1,0:T(8,128)}) %reduce-scatter.2.cloned.1.call-update) | async-done | bytes 524304 | tf_op jit(solution)/shard_map/reduce_scatter | solution.py:24
  373.9 1.8 convert_element_type.3
Async XLA Ops:
  8.0 89.9 %copy-start = (bf16[512,3328]{1,0:T(8,128)(2,1)S(1)}, bf16[512,3328]{1,0:T(8,128)(2,1)}, u32[]{:S(2)}) copy-start(bf16[512,3328]{1,0:T(8,128)(2,1)} %param.5) | copy-start | bytes 10223620
  8.0 89.9 %all-gather.3.cloned.1.call-start = ((), (), s32[]{:S(2)}) async-start(), calls=%async_computation.3 | async-start | bytes 14057472 | tf_op jit(solution)/shard_map/all_gather | solution.py:15
  109.6 128.6 %all-to-all-start = ((f32[32,64,512]{2,1,0:T(8,128)}), f32[32,64,512]{2,1,0:T(8,128)}, u32[]{:S(2)}, u32[]{:S(2)}) async-start(f32[32,64,512]{2,1,0:T(8,128)} %bitcast.17), calls=%async_computation | async-start | bytes 8388608 | tf_op jit(solution)/shard_map/all_to_all | solution.py:23
  117.2 125.8 %all-gather.5.cloned.1.call-start = ((), (), s32[]{:S(2)}) async-start(), calls=%async_computation.5 | async-start | bytes 2359296 | tf_op jit(solution)/shard_map/all_gather | solution.py:13
  117.7 256.1 %reduce-scatter.2.cloned.1.call-start = ((), (), s32[]{:S(2)}) async-start(), calls=%async_computation.4 | async-start | bytes 4718592 | tf_op jit(solution)/shard_map/reduce_scatter | solution.py:24
Sparse Core Ops, SparseCore 0:
  10.7 87.1 all-gather.2
Sparse Core Ops, SparseCore 1:
  120.3 94.5 all-gather.4
  243.0 130.8 reduce-scatter.1
where the time goes:
time: 388 us; the launch traced here: 383 us
  waiting for transfers between devices  227 us (59%)
  blocking collectives  100 us (26%)
  matrix products  24.4 us (6%)
  between operations  15.5 us (4%)
  starting transfers between devices  7.7 us (2%)
  local copies, waits for them, and re-layouts  6.61 us (2%)
    all_to_all x1, waiting for transfers between devices, local(): lax.all_to_all(partial_value, 'row', split_axis=0, concat_axis=1, tiled=T...  120 us
    all_to_all x1, blocking collectives, local(): lax.all_to_all(all_features, 'row', split_axis=1, concat_axis=0, tiled=True)  100 us
    all_gather x1, waiting for transfers between devices, local(): grad_all = lax.all_gather(out_grad, 'row', axis=0, tiled=True)  89.2 us
    reduce_scatter x1, waiting for transfers between devices, local(): lax.psum_scatter(moved, 'col', scatter_dimension=1, tiled=True)  16.2 us
    dot_general x1, matrix products, local(): lax.dot_general(column_slab, grad_all, (((0,), (0,)), ((), ())), preferre...  12.8 us
    dot_general x1, matrix products, local(): lax.dot_general(grad_all, up_weight, (((1,), (1,)), ((), ())), preferred_...  11.7 us
  transfers between devices with their start and end apart: 4, of which 3 were waited for; matrix products, arithmetic and copies ran while one was open for 5% of the time, Pallas kernels for 0%

commit v1 on v0

v1 whole, which is shorter than its diff:
```python
import math

import jax
import jax.numpy as jnp
from jax import lax
from jax.experimental import pallas as pl
from jax.experimental.pallas import tpu as pltpu
from jax.sharding import PartitionSpec as P


def move(a, f):
    pairs = []
    for z in range(4):
        for x in range(4):
            for k in range(2):
                for y in range(4):
                    for h in range(2):
                        z2, x2, k2, y2, h2 = f(z, x, k, y, h)
                        src = (z * 8 + x * 2 + k) * 8 + y * 2 + h
                        dst = (z2 * 8 + x2 * 2 + k2) * 8 + y2 * 2 + h2
                        pairs.append((src, dst))
    return lax.ppermute(a, ("row", "col"), pairs)


def to_core(a):
    return move(a, lambda z, x, k, y, h: (z, x, 1 - k, y, h))


def to_h(a):
    return move(a, lambda z, x, k, y, h: (z, x, k, y, 1 - h))


FIRST, SECOND = (1, 3), (3, 1)


def to_y(a, step):
    return move(a, lambda z, x, k, y, h: (z, x, k, y ^ step[k], h))


def swap(a, dv):
    return move(a, lambda z, x, k, y, h: (y, 2 * h + ((x & 1) ^ dv), k, z ^ y, x >> 1))


def swap_back(a, dv):
    return move(a, lambda z, x, k, y, h: (z ^ y, 2 * h + ((x & 1) ^ dv), k, z, x >> 1))


def most_of(a):
    for f in (
        lambda z, x, k, y, h: (z, x, 1 - k, y, h),
        lambda z, x, k, y, h: (z, x ^ 1, k, y, h),
        lambda z, x, k, y, h: (z ^ 1, x, k, y, h),
        lambda z, x, k, y, h: (z, x, k, y ^ 1, h),
        lambda z, x, k, y, h: (z, x ^ 2, k, y, h),
        lambda z, x, k, y, h: (z ^ 2, x, k, y, h),
        lambda z, x, k, y, h: (z, x, k, y ^ 2, h),
        lambda z, x, k, y, h: (z, x, k, y, 1 - h),
    ):
        a = jnp.maximum(a, move(a, f))
    return a


def pick(a, i):
    return lax.dynamic_index_in_dim(a, i, 0, keepdims=False)


def pack(a, scale):
    return (a * scale).astype(jnp.float16)


def partial(grad, up_weight, order, tokens):
    step = tokens // 2
    n, k = up_weight.shape

    def kernel(order_ref, g_ref, w_ref, o_ref):
        o_ref[...] = lax.dot_general(
            g_ref[...], w_ref[...], (((1,), (1,)), ((), ())), preferred_element_type=jnp.float32
        )

    return pl.pallas_call(
        kernel,
        grid_spec=pltpu.PrefetchScalarGridSpec(
            num_scalar_prefetch=1,
            grid=(order.shape[0], 2),
            in_specs=[
                pl.BlockSpec((step, k), lambda i, j, order: (order[i] * 2 + j, 0)),
                pl.BlockSpec(memory_space=pltpu.VMEM),
            ],
            out_specs=pl.BlockSpec((step, n), lambda i, j, order: (i * 2 + j, 0)),
        ),
        out_shape=jax.ShapeDtypeStruct((order.shape[0] * tokens, n), jnp.float32),
        compiler_params=pltpu.CompilerParams(vmem_limit_bytes=54 * 1024 * 1024),
    )(order, grad, up_weight)


def local(layer_input, out_grad, up_weight):
    row = lax.axis_index("row")
    col = lax.axis_index("col")
    xl, core = row // 2 % 2, row % 2
    y, h = col // 2, col % 2
    first = core == 0
    own = row // 8 ^ y
    tokens, feats = layer_input.shape
    sub = feats // 4

    grad = lax.all_gather(out_grad, "row", axis=0, tiled=True)

    pieces = layer_input.reshape(tokens, 4, sub)
    piece = [
        [lax.dynamic_index_in_dim(pieces, 2 * v + (core ^ e), 1, keepdims=False) for e in range(2)]
        for v in range(2)
    ]
    mine = jnp.stack([piece[0][0], piece[1][0]])
    other = to_core(jnp.stack([piece[0][1], piece[1][1]]))
    both = jnp.where(first, jnp.stack([mine, other], 1), jnp.stack([other, mine], 1))
    got = [swap(pick(both, xl ^ dv), dv) for dv in range(2)]
    slab = jnp.stack([pick(jnp.stack(got), xl ^ v) for v in range(2)])
    slab = jnp.stack([slab, to_h(slab)])
    slab = jnp.stack([pick(slab, h ^ v) for v in range(2)])
    slab = jnp.stack([slab, to_y(slab, FIRST)])
    far = to_y(slab, SECOND)
    slab = jnp.stack(
        [slab[0], jnp.where(first, slab[1], far[0]), far[1], jnp.where(first, far[0], slab[1])]
    )
    slab = jnp.stack([pick(slab, own ^ v) for v in range(4)]).reshape(32 * tokens, sub)

    most = [jnp.max(jnp.abs(a)).astype(jnp.float32) for a in (out_grad, up_weight)]
    most = most_of(jnp.concatenate([jnp.broadcast_to(a, (8, 128)) for a in most]))
    most = most[:1, :1] * most[8:9, :1] * (4.0 * up_weight.shape[1])
    power = jnp.clip(14.0 - jnp.ceil(jnp.log2(most)), -126.0, 126.0)
    scale, back_scale = jnp.exp2(power), jnp.exp2(-power)

    grad, slab, scale = lax.optimization_barrier((grad, slab, scale))
    near = jnp.where(first, 1, 3)
    theirs = partial(grad, up_weight, jnp.stack([own ^ near, own ^ 2]), 8 * tokens)
    mine = partial(grad, up_weight, jnp.stack([own, own ^ near ^ 2]), 8 * tokens)

    def half(a, dv):
        a = a.reshape(2, 2, 2, 2 * tokens, sub)
        return lax.dynamic_index_in_dim(a, xl ^ dv, 2, keepdims=False)

    sums = []
    for dv in range(2):
        came = to_y(pack(half(theirs, dv), scale), FIRST).astype(jnp.float32) * back_scale
        keep = half(mine, dv) + came
        came = to_y(pack(keep[1], scale), SECOND).astype(jnp.float32) * back_scale
        sums.append(keep[0] + came)
    came = [to_h(pack(pick(a, 1 - h), scale)).astype(jnp.float32) * back_scale for a in sums]
    weight_grad = lax.dot_general(
        slab, grad, (((0,), (0,)), ((), ())), preferred_element_type=jnp.float32
    )
    weight_grad = weight_grad * (1.0 / math.sqrt(tokens * 32))
    back = []
    for dv in range(2):
        total = (pick(sums[dv], h) + came[dv]).astype(jnp.bfloat16).reshape(2, tokens, sub)
        other = to_core(pick(total, 1 - core))
        kept = pick(total, core)
        both = jnp.where(first, jnp.stack([kept, other]), jnp.stack([other, kept]))
        back.append(swap_back(both, dv))
    back = jnp.stack(back)
    back = jnp.stack([pick(back, xl ^ v) for v in range(2)])
    input_grad = jnp.concatenate([back[v, e] for v in range(2) for e in range(2)], axis=1)
    return (input_grad, weight_grad)


def solution(mesh):
    in_specs = (P("row", "col"), P("row", "col"), P("row", "col"))
    out_specs = (P("row", "col"), P("row", "col"))
    return jax.shard_map(local, mesh=mesh, in_specs=in_specs, out_specs=out_specs, check_vma=False)
```

time: 388 us -> 211 us (0.54)
  waiting for transfers between devices: 227 us -> 56.6 us
  blocking collectives: 100 us -> 0 us
  starting transfers between devices: 7.7 us -> 89.5 us
  Pallas kernels: 0 us -> 18 us
  matrix products: 24.4 us -> 12.8 us
  other arithmetic: 1.77 us -> 10.9 us
    all_to_all x1 -> x0, waiting for transfers between devices: 120 us -> none  [local(): lax.all_to_all(partial_value, 'row', split_axis=0, concat_axis=1, tiled=T...]
    all_to_all x1 -> x0, blocking collectives: 100 us -> none  [local(): lax.all_to_all(all_features, 'row', split_axis=1, concat_axis=0, tiled=True)]
    ppermute x0 -> x24, starting transfers between devices: none -> 89.5 us  [move(): return lax.ppermute(a, ('row', 'col'), pairs)]
    all_gather x2 -> x1, waiting for transfers between devices: 89.2 us -> 0.87 us  [local(): grad = lax.all_gather(out_grad, 'row', axis=0, tiled=True)]
    ppermute x0 -> x24, waiting for transfers between devices: none -> 55.1 us  [move(): return lax.ppermute(a, ('row', 'col'), pairs)]
    pallas_call x0 -> x2, Pallas kernels: none -> 18 us  [partial(): pl.pallas_call(kernel, grid_spec=pltpu.PrefetchScalarGridSpec(num_scalar_...]
    reduce_scatter x1 -> x0, waiting for transfers between devices: 16.2 us -> none  [local(): lax.psum_scatter(moved, 'col', scatter_dimension=1, tiled=True)]
    dot_general x2 -> x1, matrix products: 24.4 us -> 12.8 us  [local(): lax.dot_general(slab, grad, (((0,), (0,)), ((), ())), preferred_element_t...]
  transfers between devices with their start and end apart: 4 -> 25, of which waited for: 3 -> 16; matrix products, arithmetic and copies ran while one was open for 5% -> 11% of each run, Pallas kernels for 0% -> 4%
where the time goes in v1:
time: 211 us; the launch traced here: 208 us
  starting transfers between devices  89.5 us (42%)
  waiting for transfers between devices  56.6 us (27%)
  Pallas kernels  18 us (9%)
  between operations  15.9 us (8%)
  matrix products  12.8 us (6%)
  other arithmetic  10.9 us (5%)
  local copies, waits for them, and re-layouts  4.06 us (2%)
    ppermute x24, starting transfers between devices, move(): return lax.ppermute(a, ('row', 'col'), pairs)  89.5 us
    ppermute x24, waiting for transfers between devices, move(): return lax.ppermute(a, ('row', 'col'), pairs)  55.1 us
    pallas_call x2, Pallas kernels, partial(): pl.pallas_call(kernel, grid_spec=pltpu.PrefetchScalarGridSpec(num_scalar_...  18 us
    dot_general x1, matrix products, local(): lax.dot_general(slab, grad, (((0,), (0,)), ((), ())), preferred_element_t...  12.8 us
  transfers between devices with their start and end apart: 25, of which 16 were waited for; matrix products, arithmetic and copies ran while one was open for 11% of the time, Pallas kernels for 4%

profile of v1, /device:TPU:7, one launch (start us, length us, event | category | flops | bytes accessed | tf_op | source)
XLA Modules:
  0.0 207.8 jit_solution(11964552864363484477)
XLA Ops:
  11.5 9.8 %collective-permute-start.1 = (bf16[2,64,512]{2,1,0:T(8,128)(2,1)S(1)}, bf16[2,64,512]{2,1,0:T(8,128)(2,1)S(1)}, u32[]{:S(2)}, u32[]{:S(2)}) collective-permute-start(bf16[2,64,512]{2,1,0:T(8,128)(2,1)S(1)} %get-tuple-element.27), channel_id=1, source_target_pairs={{0,0},{1,32},{2,66},{3,98},{4,132},{5,164},{6,198},{7,230},{8,8},{... | collective-permute-start | bytes 393224 | tf_op jit(solution)/shard_map/ppermute | solution.py:22
  21.4 3.2 %collective-permute-done.1 = bf16[2,64,512]{2,1,0:T(8,128)(2,1)S(1)} collective-permute-done((bf16[2,64,512]{2,1,0:T(8,128)(2,1)S(1)}, bf16[2,64,512]{2,1,0:T(8,128)(2,1)S(1)}, u32[]{:S(2)}, u32[]{:S(2)}) %collective-permute-start.1) | collective-permute-done | bytes 131104 | tf_op jit(solution)/shard_map/ppermute | solution.py:22
  24.6 9.4 %collective-permute-done.2 = bf16[2,64,512]{2,1,0:T(8,128)(2,1)S(1)} collective-permute-done((bf16[2,64,512]{2,1,0:T(8,128)(2,1)S(1)}, bf16[2,64,512]{2,1,0:T(8,128)(2,1)S(1)}, u32[]{:S(2)}, u32[]{:S(2)}) %collective-permute-start.2) | collective-permute-done | bytes 131104 | tf_op jit(solution)/shard_map/ppermute | solution.py:22
  34.3 9.2 %collective-permute-done.3 = bf16[2,2,64,512]{3,2,1,0:T(8,128)(2,1)S(1)} collective-permute-done((bf16[2,2,64,512]{3,2,1,0:T(8,128)(2,1)S(1)}, bf16[2,2,64,512]{3,2,1,0:T(8,128)(2,1)S(1)}, u32[]{:S(2)}, u32[]{:S(2)}) %collective-permute-start.3) | collective-permute-done | bytes 262176 | tf_op jit(solution)/shard_map/ppermute | solution.py:22
  43.8 25.3 %collective-permute-start.4 = (bf16[2,2,2,64,512]{4,3,2,1,0:T(8,128)(2,1)S(1)}, bf16[2,2,2,64,512]{4,3,2,1,0:T(8,128)(2,1)S(1)}, u32[]{:S(2)}, u32[]{:S(2)}) collective-permute-start(bf16[2,2,2,64,512]{4,3,2,1,0:T(8,128)(2,1)S(1)} %get-tuple-element.17), channel_id=1, source_target_pairs={{0,2},{1,3},{2,0},{3,1},{4,6},{5,7},{6,4},{7,5},{8,14},{9,15},{10,... | collective-permute-start | bytes 1572872 | tf_op jit(solution)/shard_map/ppermute | solution.py:22
  69.8 5.9 %collective-permute-done.4 = bf16[2,2,2,64,512]{4,3,2,1,0:T(8,128)(2,1)S(1)} collective-permute-done((bf16[2,2,2,64,512]{4,3,2,1,0:T(8,128)(2,1)S(1)}, bf16[2,2,2,64,512]{4,3,2,1,0:T(8,128)(2,1)S(1)}, u32[]{:S(2)}, u32[]{:S(2)}) %collective-permute-start.4) | collective-permute-done | bytes 524320 | tf_op jit(solution)/shard_map/ppermute | solution.py:22
  75.8 7.0 %collective-permute-start.5 = (bf16[2,2,2,2,64,512]{5,4,3,2,1,0:T(8,128)(2,1)S(1)}, bf16[2,2,2,2,64,512]{5,4,3,2,1,0:T(8,128)(2,1)S(1)}, u32[]{:S(2)}, u32[]{:S(2)}) collective-permute-start(bf16[2,2,2,2,64,512]{5,4,3,2,1,0:T(8,128)(2,1)S(1)} %pad_maximum_fusion.2), channel_id=1, source_target_pairs={{0,6},{1,7},{2,4},{3,5},{4,2},{5,3},{6,0},{7,1},{8,10},{9,11},{10,... | collective-permute-start | bytes 3145736 | tf_op jit(solution)/shard_map/ppermute | solution.py:22
  85.3 2.6 %collective-permute-start.6 = (f32[16,128]{1,0:T(8,128)S(1)}, f32[16,128]{1,0:T(8,128)S(1)}, u32[]{:S(2)}, u32[]{:S(2)}) collective-permute-start(f32[16,128]{1,0:T(8,128)S(1)} %concatenate.9), channel_id=1, source_target_pairs={{0,8},{1,9},{2,10},{3,11},{4,12},{5,13},{6,14},{7,15},{8,0},{9,1},... | collective-permute-start | bytes 24584 | tf_op jit(solution)/shard_map/ppermute | solution.py:22
  88.9 2.9 %collective-permute-done.7 = f32[16,128]{1,0:T(8,128)S(1)} collective-permute-done((f32[16,128]{1,0:T(8,128)S(1)}, f32[16,128]{1,0:T(8,128)S(1)}, u32[]{:S(2)}, u32[]{:S(2)}) %collective-permute-start.7) | collective-permute-done | bytes 8224 | tf_op jit(solution)/shard_map/ppermute | solution.py:22
  91.8 2.9 %collective-permute-done.8 = f32[16,128]{1,0:T(8,128)S(1)} collective-permute-done((f32[16,128]{1,0:T(8,128)S(1)}, f32[16,128]{1,0:T(8,128)S(1)}, u32[]{:S(2)}, u32[]{:S(2)}) %collective-permute-start.8) | collective-permute-done | bytes 8224 | tf_op jit(solution)/shard_map/ppermute | solution.py:22
  95.9 1.7 collective-permute-done.9
  98.2 3.6 %collective-permute-done.10 = f32[16,128]{1,0:T(8,128)S(1)} collective-permute-done((f32[16,128]{1,0:T(8,128)S(1)}, f32[16,128]{1,0:T(8,128)S(1)}, u32[]{:S(2)}, u32[]{:S(2)}) %collective-permute-start.10) | collective-permute-done | bytes 8224 | tf_op jit(solution)/shard_map/ppermute | solution.py:22
  102.2 3.1 %collective-permute-done.11 = f32[16,128]{1,0:T(8,128)S(1)} collective-permute-done((f32[16,128]{1,0:T(8,128)S(1)}, f32[16,128]{1,0:T(8,128)S(1)}, u32[]{:S(2)}, u32[]{:S(2)}) %collective-permute-start.11) | collective-permute-done | bytes 8224 | tf_op jit(solution)/shard_map/ppermute | solution.py:22
  106.5 2.7 %collective-permute-done.12 = f32[16,128]{1,0:T(8,128)S(1)} collective-permute-done((f32[16,128]{1,0:T(8,128)S(1)}, f32[16,128]{1,0:T(8,128)S(1)}, u32[]{:S(2)}, u32[]{:S(2)}) %collective-permute-start.12) | collective-permute-done | bytes 8224 | tf_op jit(solution)/shard_map/ppermute | solution.py:22
  109.3 3.8 %collective-permute-start.13 = (f32[16,128]{1,0:T(8,128)S(1)}, f32[16,128]{1,0:T(8,128)S(1)}, u32[]{:S(2)}, u32[]{:S(2)}) collective-permute-start(f32[16,128]{1,0:T(8,128)S(1)} %max.36), channel_id=1, source_target_pairs={{0,1},{1,0},{2,3},{3,2},{4,5},{5,4},{6,7},{7,6},{8,9},{9,8},{10,11... | collective-permute-start | bytes 24584 | tf_op jit(solution)/shard_map/ppermute | solution.py:22
  113.7 2.1 collective-permute-done.13
  118.4 1.6 pad_maximum_fusion.1
  120.9 9.0 %shard_map.51 = f32[1024,512]{1,0:T(8,128)} custom-call(s32[2]{0:T(128)} %get-tuple-element.43.order_ref, bf16[2048,3328]{1,0:T(8,128)(2,1)} %all-gather.2.cloned.1.call-done.g_ref, bf16[512,3328]{1,0:T(8,128)(2,1)} %w_ref.3), custom_call_target="tpu_custom_call" | custom-call | tf_op jit(solution)/shard_map/pallas_call | solution.py:80
  129.9 1.4 fusion.2
  131.2 1.4 fusion.3
  132.6 3.9 %collective-permute-start.19 = (f16[2,2,128,512]{3,2,1,0:T(8,128)(2,1)S(1)}, f16[2,2,128,512]{3,2,1,0:T(8,128)(2,1)S(1)}, u32[]{:S(2)}, u32[]{:S(2)}) collective-permute-start(f16[2,2,128,512]{3,2,1,0:T(8,128)(2,1)S(1)} %fusion.2), channel_id=1, source_target_pairs={{0,2},{1,3},{2,0},{3,1},{4,6},{5,7},{6,4},{7,5},{8,14},{9,15},{10,... | collective-permute-start | bytes 1572872 | tf_op jit(solution)/shard_map/ppermute | solution.py:22
  136.7 9.0 %shard_map.50 = f32[1024,512]{1,0:T(8,128)} custom-call(s32[2]{0:T(128)} %get-tuple-element.42.order_ref, bf16[2048,3328]{1,0:T(8,128)(2,1)} %all-gather.2.cloned.1.call-done.g_ref, bf16[512,3328]{1,0:T(8,128)(2,1)} %w_ref.3), custom_call_target="tpu_custom_call" | custom-call | tf_op jit(solution)/shard_map/pallas_call | solution.py:80
  145.7 3.0 %collective-permute-done.14 = f16[2,2,128,512]{3,2,1,0:T(8,128)(2,1)S(1)} collective-permute-done((f16[2,2,128,512]{3,2,1,0:T(8,128)(2,1)S(1)}, f16[2,2,128,512]{3,2,1,0:T(8,128)(2,1)S(1)}, u32[]{:S(2)}, u32[]{:S(2)}) %collective-permute-start.14) | collective-permute-done | bytes 524320 | tf_op jit(solution)/shard_map/ppermute | solution.py:22
  148.7 1.9 bitcast_add_fusion
  150.7 2.2 %collective-permute-start.15 = (f16[2,128,512]{2,1,0:T(8,128)(2,1)S(1)}, f16[2,128,512]{2,1,0:T(8,128)(2,1)S(1)}, u32[]{:S(2)}, u32[]{:S(2)}) collective-permute-start(f16[2,128,512]{2,1,0:T(8,128)(2,1)S(1)} %fusion.8), channel_id=1, source_target_pairs={{0,6},{1,7},{2,4},{3,5},{4,2},{5,3},{6,0},{7,1},{8,10},{9,11},{10,... | collective-permute-start | bytes 786440 | tf_op jit(solution)/shard_map/ppermute | solution.py:22
  153.1 3.6 %collective-permute-done.15 = f16[2,128,512]{2,1,0:T(8,128)(2,1)S(1)} collective-permute-done((f16[2,128,512]{2,1,0:T(8,128)(2,1)S(1)}, f16[2,128,512]{2,1,0:T(8,128)(2,1)S(1)}, u32[]{:S(2)}, u32[]{:S(2)}) %collective-permute-start.15) | collective-permute-done | bytes 262176 | tf_op jit(solution)/shard_map/ppermute | solution.py:22
  156.8 6.4 %collective-permute-start.16 = (f16[128,512]{1,0:T(8,128)(2,1)S(1)}, f16[128,512]{1,0:T(8,128)(2,1)S(1)}, u32[]{:S(2)}, u32[]{:S(2)}) collective-permute-start(f16[128,512]{1,0:T(8,128)(2,1)S(1)} %fusion.14), channel_id=1, source_target_pairs={{0,1},{1,0},{2,3},{3,2},{4,5},{5,4},{6,7},{7,6},{8,9},{9,8},{10,11... | collective-permute-start | bytes 393224 | tf_op jit(solution)/shard_map/ppermute | solution.py:22
  163.4 3.0 %collective-permute-start.21 = (f16[128,512]{1,0:T(8,128)(2,1)S(1)}, f16[128,512]{1,0:T(8,128)(2,1)S(1)}, u32[]{:S(2)}, u32[]{:S(2)}) collective-permute-start(f16[128,512]{1,0:T(8,128)(2,1)S(1)} %fusion.15), channel_id=1, source_target_pairs={{0,1},{1,0},{2,3},{3,2},{4,5},{5,4},{6,7},{7,6},{8,9},{9,8},{10,11... | collective-permute-start | bytes 393224 | tf_op jit(solution)/shard_map/ppermute | solution.py:22
  166.5 7.1 %collective-permute-start.17 = (bf16[64,512]{1,0:T(8,128)(2,1)S(1)}, bf16[64,512]{1,0:T(8,128)(2,1)S(1)}, u32[]{:S(2)}, u32[]{:S(2)}) collective-permute-start(bf16[64,512]{1,0:T(8,128)(2,1)S(1)} %get-tuple-element.39), channel_id=1, source_target_pairs={{0,8},{1,9},{2,10},{3,11},{4,12},{5,13},{6,14},{7,15},{8,0},{9,1},... | collective-permute-start | bytes 196616 | tf_op jit(solution)/shard_map/ppermute | solution.py:22
  173.6 3.3 %collective-permute-start.22 = (bf16[64,512]{1,0:T(8,128)(2,1)S(1)}, bf16[64,512]{1,0:T(8,128)(2,1)S(1)}, u32[]{:S(2)}, u32[]{:S(2)}) collective-permute-start(bf16[64,512]{1,0:T(8,128)(2,1)S(1)} %get-tuple-element.37), channel_id=1, source_target_pairs={{0,8},{1,9},{2,10},{3,11},{4,12},{5,13},{6,14},{7,15},{8,0},{9,1},... | collective-permute-start | bytes 196616 | tf_op jit(solution)/shard_map/ppermute | solution.py:22
  176.9 9.6 %collective-permute-start.18 = (bf16[2,64,512]{2,1,0:T(8,128)(2,1)S(1)}, bf16[2,64,512]{2,1,0:T(8,128)(2,1)S(1)}, u32[]{:S(2)}, u32[]{:S(2)}) collective-permute-start(bf16[2,64,512]{2,1,0:T(8,128)(2,1)S(1)} %maximum_select_fusion.1), channel_id=1, source_target_pairs={{0,0},{1,32},{2,64},{3,96},{4,128},{5,160},{6,192},{7,224},{8,8},{... | collective-permute-start | bytes 393224 | tf_op jit(solution)/shard_map/ppermute | solution.py:22
  187.3 12.8 %convolution_multiply_fusion = f32[512,3328]{1,0:T(8,128)} fusion(bf16[2048,512]{1,0:T(8,128)(2,1)S(1)} %bitcast.109, bf16[2048,3328]{1,0:T(8,128)(2,1)} %all-gather.2.cloned.1.call-done.g_ref), kind=kOutput, calls=%fused_computation | convolution fusion | flops 6981025792 | bytes 22544384 | tf_op jit(solution)/shard_map/dot_general | solution.py:149
  (84 shorter events, 17.4 us)
Async XLA Ops:
  7.2 113.7 %all-gather.2.cloned.1.call-start = ((), (), s32[]{:S(2)}) async-start(), calls=%async_computation | async-start | bytes 14057472 | tf_op jit(solution)/shard_map/all_gather | solution.py:106
  9.7 1.7 collective-permute-start
  11.5 57.6 %copy-start.4 = (bf16[64,3328]{1,0:T(8,128)(2,1)S(1)}, bf16[64,3328]{1,0:T(8,128)(2,1)}, u32[]{:S(2)}) copy-start(bf16[64,3328]{1,0:T(8,128)(2,1)} %param.4) | copy-start | bytes 1277956
  11.5 13.1 %collective-permute-start.1 = (bf16[2,64,512]{2,1,0:T(8,128)(2,1)S(1)}, bf16[2,64,512]{2,1,0:T(8,128)(2,1)S(1)}, u32[]{:S(2)}, u32[]{:S(2)}) collective-permute-start(bf16[2,64,512]{2,1,0:T(8,128)(2,1)S(1)} %get-tuple-element.27), channel_id=1, source_target_pairs={{0,0},{1,32},{2,66},{3,98},{4,132},{5,164},{6,198},{7,230},{8,8},{... | collective-permute-start | bytes 393224 | tf_op jit(solution)/shard_map/ppermute | solution.py:22
  21.3 12.7 %collective-permute-start.2 = (bf16[2,64,512]{2,1,0:T(8,128)(2,1)S(1)}, bf16[2,64,512]{2,1,0:T(8,128)(2,1)S(1)}, u32[]{:S(2)}, u32[]{:S(2)}) collective-permute-start(bf16[2,64,512]{2,1,0:T(8,128)(2,1)S(1)} %get-tuple-element.26), channel_id=1, source_target_pairs={{0,16},{1,48},{2,82},{3,114},{4,148},{5,180},{6,214},{7,246},{8,24... | collective-permute-start | bytes 393224 | tf_op jit(solution)/shard_map/ppermute | solution.py:22
  34.2 9.3 %collective-permute-start.3 = (bf16[2,2,64,512]{3,2,1,0:T(8,128)(2,1)S(1)}, bf16[2,2,64,512]{3,2,1,0:T(8,128)(2,1)S(1)}, u32[]{:S(2)}, u32[]{:S(2)}) collective-permute-start(bf16[2,2,64,512]{3,2,1,0:T(8,128)(2,1)S(1)} %get-tuple-element.22), channel_id=1, source_target_pairs={{0,1},{1,0},{2,3},{3,2},{4,5},{5,4},{6,7},{7,6},{8,9},{9,8},{10,11... | collective-permute-start | bytes 786440 | tf_op jit(solution)/shard_map/ppermute | solution.py:22
  43.7 39.1 %copy-start = (bf16[512,3328]{1,0:T(8,128)(2,1)S(1)}, bf16[512,3328]{1,0:T(8,128)(2,1)}, u32[]{:S(2)}) copy-start(bf16[512,3328]{1,0:T(8,128)(2,1)} %w_ref.3) | copy-start | bytes 10223620
  43.8 31.9 %copy-start.1 = (bf16[1,2,2,2,64,512]{5,4,3,2,1,0:T(8,128)(2,1)}, bf16[1,2,2,2,64,512]{5,4,3,2,1,0:T(8,128)(2,1)S(1)}, u32[]{:S(2)}) copy-start(bf16[1,2,2,2,64,512]{5,4,3,2,1,0:T(8,128)(2,1)S(1)} %get-tuple-element.16) | copy-start | bytes 1572868
  43.8 31.9 %collective-permute-start.4 = (bf16[2,2,2,64,512]{4,3,2,1,0:T(8,128)(2,1)S(1)}, bf16[2,2,2,64,512]{4,3,2,1,0:T(8,128)(2,1)S(1)}, u32[]{:S(2)}, u32[]{:S(2)}) collective-permute-start(bf16[2,2,2,64,512]{4,3,2,1,0:T(8,128)(2,1)S(1)} %get-tuple-element.17), channel_id=1, source_target_pairs={{0,2},{1,3},{2,0},{3,1},{4,6},{5,7},{6,4},{7,5},{8,14},{9,15},{10,... | collective-permute-start | bytes 1572872 | tf_op jit(solution)/shard_map/ppermute | solution.py:22
  75.8 41.9 %collective-permute-start.5 = (bf16[2,2,2,2,64,512]{5,4,3,2,1,0:T(8,128)(2,1)S(1)}, bf16[2,2,2,2,64,512]{5,4,3,2,1,0:T(8,128)(2,1)S(1)}, u32[]{:S(2)}, u32[]{:S(2)}) collective-permute-start(bf16[2,2,2,2,64,512]{5,4,3,2,1,0:T(8,128)(2,1)S(1)} %pad_maximum_fusion.2), channel_id=1, source_target_pairs={{0,6},{1,7},{2,4},{3,5},{4,2},{5,3},{6,0},{7,1},{8,10},{9,11},{10,... | collective-permute-start | bytes 3145736 | tf_op jit(solution)/shard_map/ppermute | solution.py:22
  83.9 34.0 %copy-start.2 = (bf16[1,2,2,2,64,512]{5,4,3,2,1,0:T(8,128)(2,1)S(1)}, bf16[1,2,2,2,64,512]{5,4,3,2,1,0:T(8,128)(2,1)}, u32[]{:S(2)}) copy-start(bf16[1,2,2,2,64,512]{5,4,3,2,1,0:T(8,128)(2,1)} %copy-done.1) | copy-start | bytes 1572868
  85.3 3.5 %collective-permute-start.6 = (f32[16,128]{1,0:T(8,128)S(1)}, f32[16,128]{1,0:T(8,128)S(1)}, u32[]{:S(2)}, u32[]{:S(2)}) collective-permute-start(f32[16,128]{1,0:T(8,128)S(1)} %concatenate.9), channel_id=1, source_target_pairs={{0,8},{1,9},{2,10},{3,11},{4,12},{5,13},{6,14},{7,15},{8,0},{9,1},... | collective-permute-start | bytes 24584 | tf_op jit(solution)/shard_map/ppermute | solution.py:22
  88.9 2.9 %collective-permute-start.7 = (f32[16,128]{1,0:T(8,128)S(1)}, f32[16,128]{1,0:T(8,128)S(1)}, u32[]{:S(2)}, u32[]{:S(2)}) collective-permute-start(f32[16,128]{1,0:T(8,128)S(1)} %broadcast_maximum_fusion), channel_id=1, source_target_pairs={{0,16},{1,17},{2,18},{3,19},{4,20},{5,21},{6,22},{7,23},{8,24},{9,... | collective-permute-start | bytes 24584 | tf_op jit(solution)/shard_map/ppermute | solution.py:22
  91.8 2.9 %collective-permute-start.8 = (f32[16,128]{1,0:T(8,128)S(1)}, f32[16,128]{1,0:T(8,128)S(1)}, u32[]{:S(2)}, u32[]{:S(2)}) collective-permute-start(f32[16,128]{1,0:T(8,128)S(1)} %fusion.25), channel_id=1, source_target_pairs={{0,64},{1,65},{2,66},{3,67},{4,68},{5,69},{6,70},{7,71},{8,72},{9,... | collective-permute-start | bytes 24584 | tf_op jit(solution)/shard_map/ppermute | solution.py:22
  94.7 2.9 %collective-permute-start.9 = (f32[16,128]{1,0:T(8,128)S(1)}, f32[16,128]{1,0:T(8,128)S(1)}, u32[]{:S(2)}, u32[]{:S(2)}) collective-permute-start(f32[16,128]{1,0:T(8,128)S(1)} %max.32), channel_id=1, source_target_pairs={{0,2},{1,3},{2,0},{3,1},{4,6},{5,7},{6,4},{7,5},{8,10},{9,11},{10,... | collective-permute-start | bytes 24584 | tf_op jit(solution)/shard_map/ppermute | solution.py:22
  97.6 4.1 %collective-permute-start.10 = (f32[16,128]{1,0:T(8,128)S(1)}, f32[16,128]{1,0:T(8,128)S(1)}, u32[]{:S(2)}, u32[]{:S(2)}) collective-permute-start(f32[16,128]{1,0:T(8,128)S(1)} %max.33), channel_id=1, source_target_pairs={{0,32},{1,33},{2,34},{3,35},{4,36},{5,37},{6,38},{7,39},{8,40},{9,... | collective-permute-start | bytes 24584 | tf_op jit(solution)/shard_map/ppermute | solution.py:22
  101.7 3.5 %collective-permute-start.11 = (f32[16,128]{1,0:T(8,128)S(1)}, f32[16,128]{1,0:T(8,128)S(1)}, u32[]{:S(2)}, u32[]{:S(2)}) collective-permute-start(f32[16,128]{1,0:T(8,128)S(1)} %max.34), channel_id=1, source_target_pairs={{0,128},{1,129},{2,130},{3,131},{4,132},{5,133},{6,134},{7,135},{8... | collective-permute-start | bytes 24584 | tf_op jit(solution)/shard_map/ppermute | solution.py:22
  105.2 4.0 %collective-permute-start.12 = (f32[16,128]{1,0:T(8,128)S(1)}, f32[16,128]{1,0:T(8,128)S(1)}, u32[]{:S(2)}, u32[]{:S(2)}) collective-permute-start(f32[16,128]{1,0:T(8,128)S(1)} %max.35), channel_id=1, source_target_pairs={{0,4},{1,5},{2,6},{3,7},{4,0},{5,1},{6,2},{7,3},{8,12},{9,13},{10,... | collective-permute-start | bytes 24584 | tf_op jit(solution)/shard_map/ppermute | solution.py:22
  109.3 6.6 %collective-permute-start.13 = (f32[16,128]{1,0:T(8,128)S(1)}, f32[16,128]{1,0:T(8,128)S(1)}, u32[]{:S(2)}, u32[]{:S(2)}) collective-permute-start(f32[16,128]{1,0:T(8,128)S(1)} %max.36), channel_id=1, source_target_pairs={{0,1},{1,0},{2,3},{3,2},{4,5},{5,4},{6,7},{7,6},{8,9},{9,8},{10,11... | collective-permute-start | bytes 24584 | tf_op jit(solution)/shard_map/ppermute | solution.py:22
  132.6 13.1 %collective-permute-start.19 = (f16[2,2,128,512]{3,2,1,0:T(8,128)(2,1)S(1)}, f16[2,2,128,512]{3,2,1,0:T(8,128)(2,1)S(1)}, u32[]{:S(2)}, u32[]{:S(2)}) collective-permute-start(f16[2,2,128,512]{3,2,1,0:T(8,128)(2,1)S(1)} %fusion.2), channel_id=1, source_target_pairs={{0,2},{1,3},{2,0},{3,1},{4,6},{5,7},{6,4},{7,5},{8,14},{9,15},{10,... | collective-permute-start | bytes 1572872 | tf_op jit(solution)/shard_map/ppermute | solution.py:22
  136.5 12.2 %collective-permute-start.14 = (f16[2,2,128,512]{3,2,1,0:T(8,128)(2,1)S(1)}, f16[2,2,128,512]{3,2,1,0:T(8,128)(2,1)S(1)}, u32[]{:S(2)}, u32[]{:S(2)}) collective-permute-start(f16[2,2,128,512]{3,2,1,0:T(8,128)(2,1)S(1)} %fusion.3), channel_id=1, source_target_pairs={{0,2},{1,3},{2,0},{3,1},{4,6},{5,7},{6,4},{7,5},{8,14},{9,15},{10,... | collective-permute-start | bytes 1572872 | tf_op jit(solution)/shard_map/ppermute | solution.py:22
  150.7 6.0 %collective-permute-start.15 = (f16[2,128,512]{2,1,0:T(8,128)(2,1)S(1)}, f16[2,128,512]{2,1,0:T(8,128)(2,1)S(1)}, u32[]{:S(2)}, u32[]{:S(2)}) collective-permute-start(f16[2,128,512]{2,1,0:T(8,128)(2,1)S(1)} %fusion.8), channel_id=1, source_target_pairs={{0,6},{1,7},{2,4},{3,5},{4,2},{5,3},{6,0},{7,1},{8,10},{9,11},{10,... | collective-permute-start | bytes 786440 | tf_op jit(solution)/shard_map/ppermute | solution.py:22
  153.0 10.3 %collective-permute-start.20 = (f16[2,128,512]{2,1,0:T(8,128)(2,1)S(1)}, f16[2,128,512]{2,1,0:T(8,128)(2,1)S(1)}, u32[]{:S(2)}, u32[]{:S(2)}) collective-permute-start(f16[2,128,512]{2,1,0:T(8,128)(2,1)S(1)} %fusion.9), channel_id=1, source_target_pairs={{0,6},{1,7},{2,4},{3,5},{4,2},{5,3},{6,0},{7,1},{8,10},{9,11},{10,... | collective-permute-start | bytes 786440 | tf_op jit(solution)/shard_map/ppermute | solution.py:22
  156.8 30.5 %copy-start.3 = (bf16[4,2,2,2,64,512]{5,4,3,2,1,0:T(8,128)(2,1)S(1)}, bf16[4,2,2,2,64,512]{5,4,3,2,1,0:T(8,128)(2,1)}, u32[]{:S(2)}) copy-start(bf16[4,2,2,2,64,512]{5,4,3,2,1,0:T(8,128)(2,1)} %pad_maximum_fusion.1) | copy-start | bytes 6291460
  156.8 9.6 %collective-permute-start.16 = (f16[128,512]{1,0:T(8,128)(2,1)S(1)}, f16[128,512]{1,0:T(8,128)(2,1)S(1)}, u32[]{:S(2)}, u32[]{:S(2)}) collective-permute-start(f16[128,512]{1,0:T(8,128)(2,1)S(1)} %fusion.14), channel_id=1, source_target_pairs={{0,1},{1,0},{2,3},{3,2},{4,5},{5,4},{6,7},{7,6},{8,9},{9,8},{10,11... | collective-permute-start | bytes 393224 | tf_op jit(solution)/shard_map/ppermute | solution.py:22
  163.4 10.2 %collective-permute-start.21 = (f16[128,512]{1,0:T(8,128)(2,1)S(1)}, f16[128,512]{1,0:T(8,128)(2,1)S(1)}, u32[]{:S(2)}, u32[]{:S(2)}) collective-permute-start(f16[128,512]{1,0:T(8,128)(2,1)S(1)} %fusion.15), channel_id=1, source_target_pairs={{0,1},{1,0},{2,3},{3,2},{4,5},{5,4},{6,7},{7,6},{8,9},{9,8},{10,11... | collective-permute-start | bytes 393224 | tf_op jit(solution)/shard_map/ppermute | solution.py:22
  166.5 10.5 %collective-permute-start.17 = (bf16[64,512]{1,0:T(8,128)(2,1)S(1)}, bf16[64,512]{1,0:T(8,128)(2,1)S(1)}, u32[]{:S(2)}, u32[]{:S(2)}) collective-permute-start(bf16[64,512]{1,0:T(8,128)(2,1)S(1)} %get-tuple-element.39), channel_id=1, source_target_pairs={{0,8},{1,9},{2,10},{3,11},{4,12},{5,13},{6,14},{7,15},{8,0},{9,1},... | collective-permute-start | bytes 196616 | tf_op jit(solution)/shard_map/ppermute | solution.py:22
  173.6 12.9 %collective-permute-start.22 = (bf16[64,512]{1,0:T(8,128)(2,1)S(1)}, bf16[64,512]{1,0:T(8,128)(2,1)S(1)}, u32[]{:S(2)}, u32[]{:S(2)}) collective-permute-start(bf16[64,512]{1,0:T(8,128)(2,1)S(1)} %get-tuple-element.37), channel_id=1, source_target_pairs={{0,8},{1,9},{2,10},{3,11},{4,12},{5,13},{6,14},{7,15},{8,0},{9,1},... | collective-permute-start | bytes 196616 | tf_op jit(solution)/shard_map/ppermute | solution.py:22
  176.9 23.1 %collective-permute-start.18 = (bf16[2,64,512]{2,1,0:T(8,128)(2,1)S(1)}, bf16[2,64,512]{2,1,0:T(8,128)(2,1)S(1)}, u32[]{:S(2)}, u32[]{:S(2)}) collective-permute-start(bf16[2,64,512]{2,1,0:T(8,128)(2,1)S(1)} %maximum_select_fusion.1), channel_id=1, source_target_pairs={{0,0},{1,32},{2,64},{3,96},{4,128},{5,160},{6,192},{7,224},{8,8},{... | collective-permute-start | bytes 393224 | tf_op jit(solution)/shard_map/ppermute | solution.py:22
  186.6 13.5 %collective-permute-start.23 = (bf16[2,64,512]{2,1,0:T(8,128)(2,1)S(1)}, bf16[2,64,512]{2,1,0:T(8,128)(2,1)S(1)}, u32[]{:S(2)}, u32[]{:S(2)}) collective-permute-start(bf16[2,64,512]{2,1,0:T(8,128)(2,1)S(1)} %maximum_select_fusion.2), channel_id=1, source_target_pairs={{0,16},{1,48},{2,80},{3,112},{4,144},{5,176},{6,208},{7,240},{8,24... | collective-permute-start | bytes 393224 | tf_op jit(solution)/shard_map/ppermute | solution.py:22
Sparse Core Ops, SparseCore 0:
  9.9 110.9 all-gather.1

commit v2 on v1

--- a/solution.py
+++ b/solution.py
@@ -38,7 +38,7 @@
 
 
 def swap(a, dv):
-    return move(a, lambda z, x, k, y, h: (y, 2 * h + ((x & 1) ^ dv), k, z ^ y, x >> 1))
+    return move(a, lambda z, x, k, y, h: (z ^ y, 2 * h + ((x & 1) ^ dv), k, y, x >> 1))
 
 
 def swap_back(a, dv):
@@ -113,6 +113,7 @@
     mine = jnp.stack([piece[0][0], piece[1][0]])
     other = to_core(jnp.stack([piece[0][1], piece[1][1]]))
     both = jnp.where(first, jnp.stack([mine, other], 1), jnp.stack([other, mine], 1))
+    both = move(both, lambda z, x, k, y, h: (z, x, k, z ^ y, h))
     got = [swap(pick(both, xl ^ dv), dv) for dv in range(2)]
     slab = jnp.stack([pick(jnp.stack(got), xl ^ v) for v in range(2)])
     slab = jnp.stack([slab, to_h(slab)])

time: 211 us -> 209 us (level)
  starting transfers between devices: 89.5 us -> 77 us
  waiting for transfers between devices: 56.6 us -> 68.8 us
    ppermute x24 -> x25, starting transfers between devices: 89.5 us -> 76.9 us  [move(): return lax.ppermute(a, ('row', 'col'), pairs)]
    ppermute x24 -> x25, waiting for transfers between devices: 55.1 us -> 64.7 us  [move(): return lax.ppermute(a, ('row', 'col'), pairs)]
    all_gather x1, waiting for transfers between devices: 0.87 us -> 3.42 us  [local(): grad = lax.all_gather(out_grad, 'row', axis=0, tiled=True)]
  transfers between devices with their start and end apart: 25 -> 26, of which waited for: 16 -> 17; matrix products, arithmetic and copies ran while one was open for 11% -> 11% of each run, Pallas kernels for 4% -> 4%
where the time goes in v2:
time: 209 us; the launch traced here: 207 us
  starting transfers between devices  77 us (37%)
  waiting for transfers between devices  68.8 us (33%)
  Pallas kernels  18 us (9%)
  between operations  15.9 us (8%)
  matrix products  12.8 us (6%)
  other arithmetic  10.9 us (5%)
  local copies, waits for them, and re-layouts  3.98 us (2%)
    ppermute x25, starting transfers between devices, move(): return lax.ppermute(a, ('row', 'col'), pairs)  76.9 us
    ppermute x25, waiting for transfers between devices, move(): return lax.ppermute(a, ('row', 'col'), pairs)  64.7 us
    pallas_call x2, Pallas kernels, partial(): pl.pallas_call(kernel, grid_spec=pltpu.PrefetchScalarGridSpec(num_scalar_...  18 us
    dot_general x1, matrix products, local(): lax.dot_general(slab, grad, (((0,), (0,)), ((), ())), preferred_element_t...  12.8 us
  transfers between devices with their start and end apart: 26, of which 17 were waited for; matrix products, arithmetic and copies ran while one was open for 11% of the time, Pallas kernels for 4%

profile of v2, /device:TPU:7, one launch (start us, length us, event | category | flops | bytes accessed | tf_op | source)
XLA Modules:
  0.0 207.4 jit_solution(1850984775167258991)
XLA Ops:
  12.2 9.8 %collective-permute-start.2 = (bf16[2,64,512]{2,1,0:T(8,128)(2,1)S(1)}, bf16[2,64,512]{2,1,0:T(8,128)(2,1)S(1)}, u32[]{:S(2)}, u32[]{:S(2)}) collective-permute-start(bf16[2,64,512]{2,1,0:T(8,128)(2,1)S(1)} %get-tuple-element.27), channel_id=1, source_target_pairs={{0,0},{1,32},{2,66},{3,98},{4,132},{5,164},{6,198},{7,230},{8,8},{... | collective-permute-start | bytes 393224 | tf_op jit(solution)/shard_map/ppermute | solution.py:22
  22.1 3.2 %collective-permute-done.2 = bf16[2,64,512]{2,1,0:T(8,128)(2,1)S(1)} collective-permute-done((bf16[2,64,512]{2,1,0:T(8,128)(2,1)S(1)}, bf16[2,64,512]{2,1,0:T(8,128)(2,1)S(1)}, u32[]{:S(2)}, u32[]{:S(2)}) %collective-permute-start.2) | collective-permute-done | bytes 131104 | tf_op jit(solution)/shard_map/ppermute | solution.py:22
  25.3 10.7 %collective-permute-done.3 = bf16[2,64,512]{2,1,0:T(8,128)(2,1)S(1)} collective-permute-done((bf16[2,64,512]{2,1,0:T(8,128)(2,1)S(1)}, bf16[2,64,512]{2,1,0:T(8,128)(2,1)S(1)}, u32[]{:S(2)}, u32[]{:S(2)}) %collective-permute-start.3) | collective-permute-done | bytes 131104 | tf_op jit(solution)/shard_map/ppermute | solution.py:22
  36.3 20.8 %collective-permute-done.4 = bf16[2,2,64,512]{3,2,1,0:T(8,128)(2,1)S(1)} collective-permute-done((bf16[2,2,64,512]{3,2,1,0:T(8,128)(2,1)S(1)}, bf16[2,2,64,512]{3,2,1,0:T(8,128)(2,1)S(1)}, u32[]{:S(2)}, u32[]{:S(2)}) %collective-permute-start.4) | collective-permute-done | bytes 262176 | tf_op jit(solution)/shard_map/ppermute | solution.py:22
  57.4 13.3 %collective-permute-start.5 = (bf16[2,2,2,64,512]{4,3,2,1,0:T(8,128)(2,1)S(1)}, bf16[2,2,2,64,512]{4,3,2,1,0:T(8,128)(2,1)S(1)}, u32[]{:S(2)}, u32[]{:S(2)}) collective-permute-start(bf16[2,2,2,64,512]{4,3,2,1,0:T(8,128)(2,1)S(1)} %get-tuple-element.17), channel_id=1, source_target_pairs={{0,2},{1,3},{2,0},{3,1},{4,6},{5,7},{6,4},{7,5},{8,14},{9,15},{10,... | collective-permute-start | bytes 1572872 | tf_op jit(solution)/shard_map/ppermute | solution.py:22
  71.3 5.9 %collective-permute-done.5 = bf16[2,2,2,64,512]{4,3,2,1,0:T(8,128)(2,1)S(1)} collective-permute-done((bf16[2,2,2,64,512]{4,3,2,1,0:T(8,128)(2,1)S(1)}, bf16[2,2,2,64,512]{4,3,2,1,0:T(8,128)(2,1)S(1)}, u32[]{:S(2)}, u32[]{:S(2)}) %collective-permute-start.5) | collective-permute-done | bytes 524320 | tf_op jit(solution)/shard_map/ppermute | solution.py:22
  79.8 4.5 %collective-permute-start.7 = (f32[16,128]{1,0:T(8,128)S(1)}, f32[16,128]{1,0:T(8,128)S(1)}, u32[]{:S(2)}, u32[]{:S(2)}) collective-permute-start(f32[16,128]{1,0:T(8,128)S(1)} %concatenate.9), channel_id=1, source_target_pairs={{0,8},{1,9},{2,10},{3,11},{4,12},{5,13},{6,14},{7,15},{8,0},{9,1},... | collective-permute-start | bytes 24584 | tf_op jit(solution)/shard_map/ppermute | solution.py:22
  85.2 2.9 %collective-permute-done.8 = f32[16,128]{1,0:T(8,128)S(1)} collective-permute-done((f32[16,128]{1,0:T(8,128)S(1)}, f32[16,128]{1,0:T(8,128)S(1)}, u32[]{:S(2)}, u32[]{:S(2)}) %collective-permute-start.8) | collective-permute-done | bytes 8224 | tf_op jit(solution)/shard_map/ppermute | solution.py:22
  88.2 1.9 collective-permute-start.9
  90.1 1.6 collective-permute-done.9
  91.7 2.9 %collective-permute-done.10 = f32[16,128]{1,0:T(8,128)S(1)} collective-permute-done((f32[16,128]{1,0:T(8,128)S(1)}, f32[16,128]{1,0:T(8,128)S(1)}, u32[]{:S(2)}, u32[]{:S(2)}) %collective-permute-start.10) | collective-permute-done | bytes 8224 | tf_op jit(solution)/shard_map/ppermute | solution.py:22
  94.6 2.3 %collective-permute-start.11 = (f32[16,128]{1,0:T(8,128)S(1)}, f32[16,128]{1,0:T(8,128)S(1)}, u32[]{:S(2)}, u32[]{:S(2)}) collective-permute-start(f32[16,128]{1,0:T(8,128)S(1)} %max.33), channel_id=1, source_target_pairs={{0,32},{1,33},{2,34},{3,35},{4,36},{5,37},{6,38},{7,39},{8,40},{9,... | collective-permute-start | bytes 24584 | tf_op jit(solution)/shard_map/ppermute | solution.py:22
  96.9 1.7 collective-permute-done.11
  98.7 3.4 %collective-permute-done.12 = f32[16,128]{1,0:T(8,128)S(1)} collective-permute-done((f32[16,128]{1,0:T(8,128)S(1)}, f32[16,128]{1,0:T(8,128)S(1)}, u32[]{:S(2)}, u32[]{:S(2)}) %collective-permute-start.12) | collective-permute-done | bytes 8224 | tf_op jit(solution)/shard_map/ppermute | solution.py:22
  102.1 2.4 %collective-permute-start.13 = (f32[16,128]{1,0:T(8,128)S(1)}, f32[16,128]{1,0:T(8,128)S(1)}, u32[]{:S(2)}, u32[]{:S(2)}) collective-permute-start(f32[16,128]{1,0:T(8,128)S(1)} %max.35), channel_id=1, source_target_pairs={{0,4},{1,5},{2,6},{3,7},{4,0},{5,1},{6,2},{7,3},{8,12},{9,13},{10,... | collective-permute-start | bytes 24584 | tf_op jit(solution)/shard_map/ppermute | solution.py:22
  104.5 1.6 collective-permute-done.13
  106.1 5.5 %collective-permute-start.14 = (f32[16,128]{1,0:T(8,128)S(1)}, f32[16,128]{1,0:T(8,128)S(1)}, u32[]{:S(2)}, u32[]{:S(2)}) collective-permute-start(f32[16,128]{1,0:T(8,128)S(1)} %max.36), channel_id=1, source_target_pairs={{0,1},{1,0},{2,3},{3,2},{4,5},{5,4},{6,7},{7,6},{8,9},{9,8},{10,11... | collective-permute-start | bytes 24584 | tf_op jit(solution)/shard_map/ppermute | solution.py:22
  115.2 1.6 pad_maximum_fusion.1
  116.8 3.4 %all-gather.2.cloned.1.call-done.g_ref = bf16[2048,3328]{1,0:T(8,128)(2,1)} async-done(((bf16[64,3328]{1,0:T(8,128)(2,1)}), bf16[2048,3328]{1,0:T(8,128)(2,1)}) %all-gather.2.cloned.1.call-update) | async-done | bytes 13631504 | tf_op jit(solution)/shard_map/all_gather | solution.py:106
  120.3 9.0 %shard_map.51 = f32[1024,512]{1,0:T(8,128)} custom-call(s32[2]{0:T(128)} %get-tuple-element.43.order_ref, bf16[2048,3328]{1,0:T(8,128)(2,1)} %all-gather.2.cloned.1.call-done.g_ref, bf16[512,3328]{1,0:T(8,128)(2,1)} %w_ref.3), custom_call_target="tpu_custom_call" | custom-call | tf_op jit(solution)/shard_map/pallas_call | solution.py:80
  132.3 2.6 %collective-permute-start.15 = (f16[2,2,128,512]{3,2,1,0:T(8,128)(2,1)S(1)}, f16[2,2,128,512]{3,2,1,0:T(8,128)(2,1)S(1)}, u32[]{:S(2)}, u32[]{:S(2)}) collective-permute-start(f16[2,2,128,512]{3,2,1,0:T(8,128)(2,1)S(1)} %fusion.3), channel_id=1, source_target_pairs={{0,2},{1,3},{2,0},{3,1},{4,6},{5,7},{6,4},{7,5},{8,14},{9,15},{10,... | collective-permute-start | bytes 1572872 | tf_op jit(solution)/shard_map/ppermute | solution.py:22
  135.0 9.0 %shard_map.50 = f32[1024,512]{1,0:T(8,128)} custom-call(s32[2]{0:T(128)} %get-tuple-element.42.order_ref, bf16[2048,3328]{1,0:T(8,128)(2,1)} %all-gather.2.cloned.1.call-done.g_ref, bf16[512,3328]{1,0:T(8,128)(2,1)} %w_ref.3), custom_call_target="tpu_custom_call" | custom-call | tf_op jit(solution)/shard_map/pallas_call | solution.py:80
  144.0 3.1 %collective-permute-done.15 = f16[2,2,128,512]{3,2,1,0:T(8,128)(2,1)S(1)} collective-permute-done((f16[2,2,128,512]{3,2,1,0:T(8,128)(2,1)S(1)}, f16[2,2,128,512]{3,2,1,0:T(8,128)(2,1)S(1)}, u32[]{:S(2)}, u32[]{:S(2)}) %collective-permute-start.15) | collective-permute-done | bytes 524320 | tf_op jit(solution)/shard_map/ppermute | solution.py:22
  147.1 1.9 bitcast_add_fusion
  150.8 3.6 %collective-permute-done.16 = f16[2,128,512]{2,1,0:T(8,128)(2,1)S(1)} collective-permute-done((f16[2,128,512]{2,1,0:T(8,128)(2,1)S(1)}, f16[2,128,512]{2,1,0:T(8,128)(2,1)S(1)}, u32[]{:S(2)}, u32[]{:S(2)}) %collective-permute-start.16) | collective-permute-done | bytes 262176 | tf_op jit(solution)/shard_map/ppermute | solution.py:22
  154.6 3.9 %collective-permute-start.17 = (f16[128,512]{1,0:T(8,128)(2,1)S(1)}, f16[128,512]{1,0:T(8,128)(2,1)S(1)}, u32[]{:S(2)}, u32[]{:S(2)}) collective-permute-start(f16[128,512]{1,0:T(8,128)(2,1)S(1)} %fusion.14), channel_id=1, source_target_pairs={{0,1},{1,0},{2,3},{3,2},{4,5},{5,4},{6,7},{7,6},{8,9},{9,8},{10,11... | collective-permute-start | bytes 393224 | tf_op jit(solution)/shard_map/ppermute | solution.py:22
  158.6 2.7 %collective-permute-start.22 = (f16[128,512]{1,0:T(8,128)(2,1)S(1)}, f16[128,512]{1,0:T(8,128)(2,1)S(1)}, u32[]{:S(2)}, u32[]{:S(2)}) collective-permute-start(f16[128,512]{1,0:T(8,128)(2,1)S(1)} %fusion.15), channel_id=1, source_target_pairs={{0,1},{1,0},{2,3},{3,2},{4,5},{5,4},{6,7},{7,6},{8,9},{9,8},{10,11... | collective-permute-start | bytes 393224 | tf_op jit(solution)/shard_map/ppermute | solution.py:22
  162.4 7.8 %collective-permute-start.18 = (bf16[64,512]{1,0:T(8,128)(2,1)S(1)}, bf16[64,512]{1,0:T(8,128)(2,1)S(1)}, u32[]{:S(2)}, u32[]{:S(2)}) collective-permute-start(bf16[64,512]{1,0:T(8,128)(2,1)S(1)} %get-tuple-element.39), channel_id=1, source_target_pairs={{0,8},{1,9},{2,10},{3,11},{4,12},{5,13},{6,14},{7,15},{8,0},{9,1},... | collective-permute-start | bytes 196616 | tf_op jit(solution)/shard_map/ppermute | solution.py:22
  170.3 5.8 %collective-permute-start.23 = (bf16[64,512]{1,0:T(8,128)(2,1)S(1)}, bf16[64,512]{1,0:T(8,128)(2,1)S(1)}, u32[]{:S(2)}, u32[]{:S(2)}) collective-permute-start(bf16[64,512]{1,0:T(8,128)(2,1)S(1)} %get-tuple-element.37), channel_id=1, source_target_pairs={{0,8},{1,9},{2,10},{3,11},{4,12},{5,13},{6,14},{7,15},{8,0},{9,1},... | collective-permute-start | bytes 196616 | tf_op jit(solution)/shard_map/ppermute | solution.py:22
  176.2 8.5 %collective-permute-start.19 = (bf16[2,64,512]{2,1,0:T(8,128)(2,1)S(1)}, bf16[2,64,512]{2,1,0:T(8,128)(2,1)S(1)}, u32[]{:S(2)}, u32[]{:S(2)}) collective-permute-start(bf16[2,64,512]{2,1,0:T(8,128)(2,1)S(1)} %maximum_select_fusion.1), channel_id=1, source_target_pairs={{0,0},{1,32},{2,64},{3,96},{4,128},{5,160},{6,192},{7,224},{8,8},{... | collective-permute-start | bytes 393224 | tf_op jit(solution)/shard_map/ppermute | solution.py:22
  184.7 2.1 %collective-permute-start.24 = (bf16[2,64,512]{2,1,0:T(8,128)(2,1)S(1)}, bf16[2,64,512]{2,1,0:T(8,128)(2,1)S(1)}, u32[]{:S(2)}, u32[]{:S(2)}) collective-permute-start(bf16[2,64,512]{2,1,0:T(8,128)(2,1)S(1)} %maximum_select_fusion.2), channel_id=1, source_target_pairs={{0,16},{1,48},{2,80},{3,112},{4,144},{5,176},{6,208},{7,240},{8,24... | collective-permute-start | bytes 393224 | tf_op jit(solution)/shard_map/ppermute | solution.py:22
  186.9 12.8 %convolution_multiply_fusion = f32[512,3328]{1,0:T(8,128)} fusion(bf16[2048,512]{1,0:T(8,128)(2,1)S(1)} %bitcast.109, bf16[2048,3328]{1,0:T(8,128)(2,1)} %all-gather.2.cloned.1.call-done.g_ref), kind=kOutput, calls=%fused_computation | convolution fusion | flops 6981025792 | bytes 22544384 | tf_op jit(solution)/shard_map/dot_general | solution.py:150
  (86 shorter events, 19.2 us)
Async XLA Ops:
  7.2 113.1 %all-gather.2.cloned.1.call-start = ((), (), s32[]{:S(2)}) async-start(), calls=%async_computation | async-start | bytes 14057472 | tf_op jit(solution)/shard_map/all_gather | solution.py:106
  9.7 1.7 collective-permute-start
  11.5 0.7 collective-permute-start.1
  12.2 58.4 %copy-start.4 = (bf16[64,3328]{1,0:T(8,128)(2,1)S(1)}, bf16[64,3328]{1,0:T(8,128)(2,1)}, u32[]{:S(2)}) copy-start(bf16[64,3328]{1,0:T(8,128)(2,1)} %param.4) | copy-start | bytes 1277956
  12.2 13.1 %collective-permute-start.2 = (bf16[2,64,512]{2,1,0:T(8,128)(2,1)S(1)}, bf16[2,64,512]{2,1,0:T(8,128)(2,1)S(1)}, u32[]{:S(2)}, u32[]{:S(2)}) collective-permute-start(bf16[2,64,512]{2,1,0:T(8,128)(2,1)S(1)} %get-tuple-element.27), channel_id=1, source_target_pairs={{0,0},{1,32},{2,66},{3,98},{4,132},{5,164},{6,198},{7,230},{8,8},{... | collective-permute-start | bytes 393224 | tf_op jit(solution)/shard_map/ppermute | solution.py:22
  22.0 14.0 %collective-permute-start.3 = (bf16[2,64,512]{2,1,0:T(8,128)(2,1)S(1)}, bf16[2,64,512]{2,1,0:T(8,128)(2,1)S(1)}, u32[]{:S(2)}, u32[]{:S(2)}) collective-permute-start(bf16[2,64,512]{2,1,0:T(8,128)(2,1)S(1)} %get-tuple-element.26), channel_id=1, source_target_pairs={{0,16},{1,48},{2,82},{3,114},{4,148},{5,180},{6,214},{7,246},{8,24... | collective-permute-start | bytes 393224 | tf_op jit(solution)/shard_map/ppermute | solution.py:22
  36.2 20.9 %collective-permute-start.4 = (bf16[2,2,64,512]{3,2,1,0:T(8,128)(2,1)S(1)}, bf16[2,2,64,512]{3,2,1,0:T(8,128)(2,1)S(1)}, u32[]{:S(2)}, u32[]{:S(2)}) collective-permute-start(bf16[2,2,64,512]{3,2,1,0:T(8,128)(2,1)S(1)} %get-tuple-element.22), channel_id=1, source_target_pairs={{0,1},{1,0},{2,3},{3,2},{4,5},{5,4},{6,7},{7,6},{8,9},{9,8},{10,11... | collective-permute-start | bytes 786440 | tf_op jit(solution)/shard_map/ppermute | solution.py:22
  57.3 20.2 %copy-start = (bf16[512,3328]{1,0:T(8,128)(2,1)S(1)}, bf16[512,3328]{1,0:T(8,128)(2,1)}, u32[]{:S(2)}) copy-start(bf16[512,3328]{1,0:T(8,128)(2,1)} %w_ref.3) | copy-start | bytes 10223620
  57.3 19.9 %copy-start.1 = (bf16[1,2,2,2,64,512]{5,4,3,2,1,0:T(8,128)(2,1)}, bf16[1,2,2,2,64,512]{5,4,3,2,1,0:T(8,128)(2,1)S(1)}, u32[]{:S(2)}) copy-start(bf16[1,2,2,2,64,512]{5,4,3,2,1,0:T(8,128)(2,1)S(1)} %get-tuple-element.16) | copy-start | bytes 1572868
  57.4 19.9 %collective-permute-start.5 = (bf16[2,2,2,64,512]{4,3,2,1,0:T(8,128)(2,1)S(1)}, bf16[2,2,2,64,512]{4,3,2,1,0:T(8,128)(2,1)S(1)}, u32[]{:S(2)}, u32[]{:S(2)}) collective-permute-start(bf16[2,2,2,64,512]{4,3,2,1,0:T(8,128)(2,1)S(1)} %get-tuple-element.17), channel_id=1, source_target_pairs={{0,2},{1,3},{2,0},{3,1},{4,6},{5,7},{6,4},{7,5},{8,14},{9,15},{10,... | collective-permute-start | bytes 1572872 | tf_op jit(solution)/shard_map/ppermute | solution.py:22
  77.3 37.3 %collective-permute-start.6 = (bf16[2,2,2,2,64,512]{5,4,3,2,1,0:T(8,128)(2,1)S(1)}, bf16[2,2,2,2,64,512]{5,4,3,2,1,0:T(8,128)(2,1)S(1)}, u32[]{:S(2)}, u32[]{:S(2)}) collective-permute-start(bf16[2,2,2,2,64,512]{5,4,3,2,1,0:T(8,128)(2,1)S(1)} %pad_maximum_fusion.2), channel_id=1, source_target_pairs={{0,6},{1,7},{2,4},{3,5},{4,2},{5,3},{6,0},{7,1},{8,10},{9,11},{10,... | collective-permute-start | bytes 3145736 | tf_op jit(solution)/shard_map/ppermute | solution.py:22
  78.5 36.3 %copy-start.2 = (bf16[1,2,2,2,64,512]{5,4,3,2,1,0:T(8,128)(2,1)S(1)}, bf16[1,2,2,2,64,512]{5,4,3,2,1,0:T(8,128)(2,1)}, u32[]{:S(2)}) copy-start(bf16[1,2,2,2,64,512]{5,4,3,2,1,0:T(8,128)(2,1)} %copy-done.1) | copy-start | bytes 1572868
  79.8 5.3 %collective-permute-start.7 = (f32[16,128]{1,0:T(8,128)S(1)}, f32[16,128]{1,0:T(8,128)S(1)}, u32[]{:S(2)}, u32[]{:S(2)}) collective-permute-start(f32[16,128]{1,0:T(8,128)S(1)} %concatenate.9), channel_id=1, source_target_pairs={{0,8},{1,9},{2,10},{3,11},{4,12},{5,13},{6,14},{7,15},{8,0},{9,1},... | collective-permute-start | bytes 24584 | tf_op jit(solution)/shard_map/ppermute | solution.py:22
  85.2 2.9 %collective-permute-start.8 = (f32[16,128]{1,0:T(8,128)S(1)}, f32[16,128]{1,0:T(8,128)S(1)}, u32[]{:S(2)}, u32[]{:S(2)}) collective-permute-start(f32[16,128]{1,0:T(8,128)S(1)} %broadcast_maximum_fusion), channel_id=1, source_target_pairs={{0,16},{1,17},{2,18},{3,19},{4,20},{5,21},{6,22},{7,23},{8,24},{9,... | collective-permute-start | bytes 24584 | tf_op jit(solution)/shard_map/ppermute | solution.py:22
  88.2 3.5 %collective-permute-start.9 = (f32[16,128]{1,0:T(8,128)S(1)}, f32[16,128]{1,0:T(8,128)S(1)}, u32[]{:S(2)}, u32[]{:S(2)}) collective-permute-start(f32[16,128]{1,0:T(8,128)S(1)} %fusion.25), channel_id=1, source_target_pairs={{0,64},{1,65},{2,66},{3,67},{4,68},{5,69},{6,70},{7,71},{8,72},{9,... | collective-permute-start | bytes 24584 | tf_op jit(solution)/shard_map/ppermute | solution.py:22
  91.7 2.9 %collective-permute-start.10 = (f32[16,128]{1,0:T(8,128)S(1)}, f32[16,128]{1,0:T(8,128)S(1)}, u32[]{:S(2)}, u32[]{:S(2)}) collective-permute-start(f32[16,128]{1,0:T(8,128)S(1)} %max.32), channel_id=1, source_target_pairs={{0,2},{1,3},{2,0},{3,1},{4,6},{5,7},{6,4},{7,5},{8,10},{9,11},{10,... | collective-permute-start | bytes 24584 | tf_op jit(solution)/shard_map/ppermute | solution.py:22
  94.6 4.0 %collective-permute-start.11 = (f32[16,128]{1,0:T(8,128)S(1)}, f32[16,128]{1,0:T(8,128)S(1)}, u32[]{:S(2)}, u32[]{:S(2)}) collective-permute-start(f32[16,128]{1,0:T(8,128)S(1)} %max.33), channel_id=1, source_target_pairs={{0,32},{1,33},{2,34},{3,35},{4,36},{5,37},{6,38},{7,39},{8,40},{9,... | collective-permute-start | bytes 24584 | tf_op jit(solution)/shard_map/ppermute | solution.py:22
  98.6 3.5 %collective-permute-start.12 = (f32[16,128]{1,0:T(8,128)S(1)}, f32[16,128]{1,0:T(8,128)S(1)}, u32[]{:S(2)}, u32[]{:S(2)}) collective-permute-start(f32[16,128]{1,0:T(8,128)S(1)} %max.34), channel_id=1, source_target_pairs={{0,128},{1,129},{2,130},{3,131},{4,132},{5,133},{6,134},{7,135},{8... | collective-permute-start | bytes 24584 | tf_op jit(solution)/shard_map/ppermute | solution.py:22
  102.1 4.0 %collective-permute-start.13 = (f32[16,128]{1,0:T(8,128)S(1)}, f32[16,128]{1,0:T(8,128)S(1)}, u32[]{:S(2)}, u32[]{:S(2)}) collective-permute-start(f32[16,128]{1,0:T(8,128)S(1)} %max.35), channel_id=1, source_target_pairs={{0,4},{1,5},{2,6},{3,7},{4,0},{5,1},{6,2},{7,3},{8,12},{9,13},{10,... | collective-permute-start | bytes 24584 | tf_op jit(solution)/shard_map/ppermute | solution.py:22
  106.1 6.6 %collective-permute-start.14 = (f32[16,128]{1,0:T(8,128)S(1)}, f32[16,128]{1,0:T(8,128)S(1)}, u32[]{:S(2)}, u32[]{:S(2)}) collective-permute-start(f32[16,128]{1,0:T(8,128)S(1)} %max.36), channel_id=1, source_target_pairs={{0,1},{1,0},{2,3},{3,2},{4,5},{5,4},{6,7},{7,6},{8,9},{9,8},{10,11... | collective-permute-start | bytes 24584 | tf_op jit(solution)/shard_map/ppermute | solution.py:22
  132.0 12.0 %collective-permute-start.20 = (f16[2,2,128,512]{3,2,1,0:T(8,128)(2,1)S(1)}, f16[2,2,128,512]{3,2,1,0:T(8,128)(2,1)S(1)}, u32[]{:S(2)}, u32[]{:S(2)}) collective-permute-start(f16[2,2,128,512]{3,2,1,0:T(8,128)(2,1)S(1)} %fusion.2), channel_id=1, source_target_pairs={{0,2},{1,3},{2,0},{3,1},{4,6},{5,7},{6,4},{7,5},{8,14},{9,15},{10,... | collective-permute-start | bytes 1572872 | tf_op jit(solution)/shard_map/ppermute | solution.py:22
  132.3 14.8 %collective-permute-start.15 = (f16[2,2,128,512]{3,2,1,0:T(8,128)(2,1)S(1)}, f16[2,2,128,512]{3,2,1,0:T(8,128)(2,1)S(1)}, u32[]{:S(2)}, u32[]{:S(2)}) collective-permute-start(f16[2,2,128,512]{3,2,1,0:T(8,128)(2,1)S(1)} %fusion.3), channel_id=1, source_target_pairs={{0,2},{1,3},{2,0},{3,1},{4,6},{5,7},{6,4},{7,5},{8,14},{9,15},{10,... | collective-permute-start | bytes 1572872 | tf_op jit(solution)/shard_map/ppermute | solution.py:22
  149.1 5.3 %collective-permute-start.16 = (f16[2,128,512]{2,1,0:T(8,128)(2,1)S(1)}, f16[2,128,512]{2,1,0:T(8,128)(2,1)S(1)}, u32[]{:S(2)}, u32[]{:S(2)}) collective-permute-start(f16[2,128,512]{2,1,0:T(8,128)(2,1)S(1)} %fusion.8), channel_id=1, source_target_pairs={{0,6},{1,7},{2,4},{3,5},{4,2},{5,3},{6,0},{7,1},{8,10},{9,11},{10,... | collective-permute-start | bytes 786440 | tf_op jit(solution)/shard_map/ppermute | solution.py:22
  149.3 9.2 %collective-permute-start.21 = (f16[2,128,512]{2,1,0:T(8,128)(2,1)S(1)}, f16[2,128,512]{2,1,0:T(8,128)(2,1)S(1)}, u32[]{:S(2)}, u32[]{:S(2)}) collective-permute-start(f16[2,128,512]{2,1,0:T(8,128)(2,1)S(1)} %fusion.9), channel_id=1, source_target_pairs={{0,6},{1,7},{2,4},{3,5},{4,2},{5,3},{6,0},{7,1},{8,10},{9,11},{10,... | collective-permute-start | bytes 786440 | tf_op jit(solution)/shard_map/ppermute | solution.py:22
  154.5 32.4 %copy-start.3 = (bf16[4,2,2,2,64,512]{5,4,3,2,1,0:T(8,128)(2,1)S(1)}, bf16[4,2,2,2,64,512]{5,4,3,2,1,0:T(8,128)(2,1)}, u32[]{:S(2)}) copy-start(bf16[4,2,2,2,64,512]{5,4,3,2,1,0:T(8,128)(2,1)} %pad_maximum_fusion.1) | copy-start | bytes 6291460
  154.6 7.8 %collective-permute-start.17 = (f16[128,512]{1,0:T(8,128)(2,1)S(1)}, f16[128,512]{1,0:T(8,128)(2,1)S(1)}, u32[]{:S(2)}, u32[]{:S(2)}) collective-permute-start(f16[128,512]{1,0:T(8,128)(2,1)S(1)} %fusion.14), channel_id=1, source_target_pairs={{0,1},{1,0},{2,3},{3,2},{4,5},{5,4},{6,7},{7,6},{8,9},{9,8},{10,11... | collective-permute-start | bytes 393224 | tf_op jit(solution)/shard_map/ppermute | solution.py:22
  158.6 11.6 %collective-permute-start.22 = (f16[128,512]{1,0:T(8,128)(2,1)S(1)}, f16[128,512]{1,0:T(8,128)(2,1)S(1)}, u32[]{:S(2)}, u32[]{:S(2)}) collective-permute-start(f16[128,512]{1,0:T(8,128)(2,1)S(1)} %fusion.15), channel_id=1, source_target_pairs={{0,1},{1,0},{2,3},{3,2},{4,5},{5,4},{6,7},{7,6},{8,9},{9,8},{10,11... | collective-permute-start | bytes 393224 | tf_op jit(solution)/shard_map/ppermute | solution.py:22
  162.4 13.7 %collective-permute-start.18 = (bf16[64,512]{1,0:T(8,128)(2,1)S(1)}, bf16[64,512]{1,0:T(8,128)(2,1)S(1)}, u32[]{:S(2)}, u32[]{:S(2)}) collective-permute-start(bf16[64,512]{1,0:T(8,128)(2,1)S(1)} %get-tuple-element.39), channel_id=1, source_target_pairs={{0,8},{1,9},{2,10},{3,11},{4,12},{5,13},{6,14},{7,15},{8,0},{9,1},... | collective-permute-start | bytes 196616 | tf_op jit(solution)/shard_map/ppermute | solution.py:22
  170.3 14.4 %collective-permute-start.23 = (bf16[64,512]{1,0:T(8,128)(2,1)S(1)}, bf16[64,512]{1,0:T(8,128)(2,1)S(1)}, u32[]{:S(2)}, u32[]{:S(2)}) collective-permute-start(bf16[64,512]{1,0:T(8,128)(2,1)S(1)} %get-tuple-element.37), channel_id=1, source_target_pairs={{0,8},{1,9},{2,10},{3,11},{4,12},{5,13},{6,14},{7,15},{8,0},{9,1},... | collective-permute-start | bytes 196616 | tf_op jit(solution)/shard_map/ppermute | solution.py:22
  176.2 23.5 %collective-permute-start.19 = (bf16[2,64,512]{2,1,0:T(8,128)(2,1)S(1)}, bf16[2,64,512]{2,1,0:T(8,128)(2,1)S(1)}, u32[]{:S(2)}, u32[]{:S(2)}) collective-permute-start(bf16[2,64,512]{2,1,0:T(8,128)(2,1)S(1)} %maximum_select_fusion.1), channel_id=1, source_target_pairs={{0,0},{1,32},{2,64},{3,96},{4,128},{5,160},{6,192},{7,224},{8,8},{... | collective-permute-start | bytes 393224 | tf_op jit(solution)/shard_map/ppermute | solution.py:22
  184.7 14.9 %collective-permute-start.24 = (bf16[2,64,512]{2,1,0:T(8,128)(2,1)S(1)}, bf16[2,64,512]{2,1,0:T(8,128)(2,1)S(1)}, u32[]{:S(2)}, u32[]{:S(2)}) collective-permute-start(bf16[2,64,512]{2,1,0:T(8,128)(2,1)S(1)} %maximum_select_fusion.2), channel_id=1, source_target_pairs={{0,16},{1,48},{2,80},{3,112},{4,144},{5,176},{6,208},{7,240},{8,24... | collective-permute-start | bytes 393224 | tf_op jit(solution)/shard_map/ppermute | solution.py:22
Sparse Core Ops, SparseCore 0:
  9.9 110.3 all-gather.1

commit v3 on v2

--- a/solution.py
+++ b/solution.py
@@ -45,18 +45,21 @@
     return move(a, lambda z, x, k, y, h: (z ^ y, 2 * h + ((x & 1) ^ dv), k, z, x >> 1))
 
 
-def most_of(a):
-    for f in (
-        lambda z, x, k, y, h: (z, x, 1 - k, y, h),
-        lambda z, x, k, y, h: (z, x ^ 1, k, y, h),
-        lambda z, x, k, y, h: (z ^ 1, x, k, y, h),
-        lambda z, x, k, y, h: (z, x, k, y ^ 1, h),
-        lambda z, x, k, y, h: (z, x ^ 2, k, y, h),
-        lambda z, x, k, y, h: (z ^ 2, x, k, y, h),
-        lambda z, x, k, y, h: (z, x, k, y ^ 2, h),
-        lambda z, x, k, y, h: (z, x, k, y, 1 - h),
-    ):
-        a = jnp.maximum(a, move(a, f))
+ROUNDS = (
+    lambda z, x, k, y, h: (z, x, 1 - k, y, h),
+    lambda z, x, k, y, h: (z, x ^ 1, k, y, h),
+    lambda z, x, k, y, h: (z, x, k, y ^ 1, h),
+    lambda z, x, k, y, h: (z, x ^ 2, k, y, h),
+    lambda z, x, k, y, h: (z, x, k, y ^ 2, h),
+    lambda z, x, k, y, h: (z ^ 1, x, k, y, h),
+    lambda z, x, k, y, h: (z ^ 2, x, k, y, h),
+    lambda z, x, k, y, h: (z, x, k, y, 1 - h),
+)
+
+
+def most_of(a, rounds):
+    for i in rounds:
+        a = jnp.maximum(a, move(a, ROUNDS[i]))
     return a
 
 
@@ -115,6 +118,9 @@
     both = jnp.where(first, jnp.stack([mine, other], 1), jnp.stack([other, mine], 1))
     both = move(both, lambda z, x, k, y, h: (z, x, k, z ^ y, h))
     got = [swap(pick(both, xl ^ dv), dv) for dv in range(2)]
+    most = [jnp.max(jnp.abs(a)).astype(jnp.float32) for a in (out_grad, up_weight)]
+    most = most_of(jnp.concatenate([jnp.broadcast_to(a, (8, 128)) for a in most]), range(3))
+    *got, most = lax.optimization_barrier((*got, most))
     slab = jnp.stack([pick(jnp.stack(got), xl ^ v) for v in range(2)])
     slab = jnp.stack([slab, to_h(slab)])
     slab = jnp.stack([pick(slab, h ^ v) for v in range(2)])
@@ -125,8 +131,7 @@
     )
     slab = jnp.stack([pick(slab, own ^ v) for v in range(4)]).reshape(32 * tokens, sub)
 
-    most = [jnp.max(jnp.abs(a)).astype(jnp.float32) for a in (out_grad, up_weight)]
-    most = most_of(jnp.concatenate([jnp.broadcast_to(a, (8, 128)) for a in most]))
+    most = most_of(most, range(3, 8))
     most = most[:1, :1] * most[8:9, :1] * (4.0 * up_weight.shape[1])
     power = jnp.clip(14.0 - jnp.ceil(jnp.log2(most)), -126.0, 126.0)
     scale, back_scale = jnp.exp2(power), jnp.exp2(-power)

time: 209 us -> 205 us (0.981)
  starting transfers between devices: 77 us -> 70.5 us
    ppermute x25, starting transfers between devices: 76.9 us -> 70.5 us  [move(): return lax.ppermute(a, ('row', 'col'), pairs)]
    all_gather x1, waiting for transfers between devices: 3.42 us -> 6.81 us  [local(): grad = lax.all_gather(out_grad, 'row', axis=0, tiled=True)]
    ppermute x25, waiting for transfers between devices: 64.7 us -> 62.5 us  [move(): return lax.ppermute(a, ('row', 'col'), pairs)]
  transfers between devices with their start and end apart: 26 -> 26, of which waited for: 17 -> 15; matrix products, arithmetic and copies ran while one was open for 11% -> 12% of each run, Pallas kernels for 4% -> 4%
where the time goes in v3:
time: 205 us; the launch traced here: 204 us
  starting transfers between devices  70.5 us (34%)
  waiting for transfers between devices  70 us (34%)
  Pallas kernels  18 us (9%)
  between operations  15.9 us (8%)
  other arithmetic  12.8 us (6%)
  matrix products  12.8 us (6%)
  local copies, waits for them, and re-layouts  3.96 us (2%)
    ppermute x25, starting transfers between devices, move(): return lax.ppermute(a, ('row', 'col'), pairs)  70.5 us
    ppermute x25, waiting for transfers between devices, move(): return lax.ppermute(a, ('row', 'col'), pairs)  62.5 us
    pallas_call x2, Pallas kernels, partial(): pl.pallas_call(kernel, grid_spec=pltpu.PrefetchScalarGridSpec(num_scalar_...  18 us
    dot_general x1, matrix products, local(): lax.dot_general(slab, grad, (((0,), (0,)), ((), ())), preferred_element_t...  12.8 us
    all_gather x1, waiting for transfers between devices, local(): grad = lax.all_gather(out_grad, 'row', axis=0, tiled=True)  6.81 us
  transfers between devices with their start and end apart: 26, of which 15 were waited for; matrix products, arithmetic and copies ran while one was open for 12% of the time, Pallas kernels for 4%

profile of v3, /device:TPU:7, one launch (start us, length us, event | category | flops | bytes accessed | tf_op | source)
XLA Modules:
  0.0 204.0 jit_solution(14979384048940584969)
XLA Ops:
  10.5 3.0 %abs_reduce_fusion = bf16[]{:T(256)} fusion(bf16[512,3328]{1,0:T(8,128)(2,1)} %w_ref.3), kind=kLoop, calls=%fused_computation.1 | loop fusion | flops 3407871 | bytes 3407874 | tf_op jit(solution)/shard_map/reduce_max | solution.py:121
  18.1 9.4 %collective-permute-start.2 = (bf16[2,64,512]{2,1,0:T(8,128)(2,1)S(1)}, bf16[2,64,512]{2,1,0:T(8,128)(2,1)S(1)}, u32[]{:S(2)}, u32[]{:S(2)}) collective-permute-start(bf16[2,64,512]{2,1,0:T(8,128)(2,1)S(1)} %get-tuple-element.33), channel_id=1, source_target_pairs={{0,0},{1,32},{2,66},{3,98},{4,132},{5,164},{6,198},{7,230},{8,8},{... | collective-permute-start | bytes 393224 | tf_op jit(solution)/shard_map/ppermute | solution.py:22
  28.3 5.8 %collective-permute-start.6 = (f32[16,128]{1,0:T(8,128)S(1)}, f32[16,128]{1,0:T(8,128)S(1)}, u32[]{:S(2)}, u32[]{:S(2)}) collective-permute-start(f32[16,128]{1,0:T(8,128)S(1)} %fusion.25), channel_id=1, source_target_pairs={{0,2},{1,3},{2,0},{3,1},{4,6},{5,7},{6,4},{7,5},{8,10},{9,11},{10,... | collective-permute-start | bytes 24584 | tf_op jit(solution)/shard_map/ppermute | solution.py:22
  34.1 1.4 collective-permute-done.6
  35.5 6.0 %collective-permute-done.3 = bf16[2,64,512]{2,1,0:T(8,128)(2,1)S(1)} collective-permute-done((bf16[2,64,512]{2,1,0:T(8,128)(2,1)S(1)}, bf16[2,64,512]{2,1,0:T(8,128)(2,1)S(1)}, u32[]{:S(2)}, u32[]{:S(2)}) %collective-permute-start.3) | collective-permute-done | bytes 131104 | tf_op jit(solution)/shard_map/ppermute | solution.py:22
  41.8 20.6 %collective-permute-done.7 = bf16[2,2,64,512]{3,2,1,0:T(8,128)(2,1)S(1)} collective-permute-done((bf16[2,2,64,512]{3,2,1,0:T(8,128)(2,1)S(1)}, bf16[2,2,64,512]{3,2,1,0:T(8,128)(2,1)S(1)}, u32[]{:S(2)}, u32[]{:S(2)}) %collective-permute-start.7) | collective-permute-done | bytes 262176 | tf_op jit(solution)/shard_map/ppermute | solution.py:22
  62.6 10.4 %collective-permute-start.8 = (bf16[2,2,2,64,512]{4,3,2,1,0:T(8,128)(2,1)S(1)}, bf16[2,2,2,64,512]{4,3,2,1,0:T(8,128)(2,1)S(1)}, u32[]{:S(2)}, u32[]{:S(2)}) collective-permute-start(bf16[2,2,2,64,512]{4,3,2,1,0:T(8,128)(2,1)S(1)} %get-tuple-element.23), channel_id=1, source_target_pairs={{0,2},{1,3},{2,0},{3,1},{4,6},{5,7},{6,4},{7,5},{8,14},{9,15},{10,... | collective-permute-start | bytes 1572872 | tf_op jit(solution)/shard_map/ppermute | solution.py:22
  73.1 6.6 %collective-permute-done.8 = bf16[2,2,2,64,512]{4,3,2,1,0:T(8,128)(2,1)S(1)} collective-permute-done((bf16[2,2,2,64,512]{4,3,2,1,0:T(8,128)(2,1)S(1)}, bf16[2,2,2,64,512]{4,3,2,1,0:T(8,128)(2,1)S(1)}, u32[]{:S(2)}, u32[]{:S(2)}) %collective-permute-start.8) | collective-permute-done | bytes 524320 | tf_op jit(solution)/shard_map/ppermute | solution.py:22
  79.9 4.0 %collective-permute-done.10 = f32[16,128]{1,0:T(8,128)S(1)} collective-permute-done((f32[16,128]{1,0:T(8,128)S(1)}, f32[16,128]{1,0:T(8,128)S(1)}, u32[]{:S(2)}, u32[]{:S(2)}) %collective-permute-start.10) | collective-permute-done | bytes 8224 | tf_op jit(solution)/shard_map/ppermute | solution.py:22
  83.9 3.8 %collective-permute-start.11 = (f32[16,128]{1,0:T(8,128)S(1)}, f32[16,128]{1,0:T(8,128)S(1)}, u32[]{:S(2)}, u32[]{:S(2)}) collective-permute-start(f32[16,128]{1,0:T(8,128)S(1)} %max.33), channel_id=1, source_target_pairs={{0,4},{1,5},{2,6},{3,7},{4,0},{5,1},{6,2},{7,3},{8,12},{9,13},{10,... | collective-permute-start | bytes 24584 | tf_op jit(solution)/shard_map/ppermute | solution.py:22
  87.7 8.5 %collective-permute-done.11 = f32[16,128]{1,0:T(8,128)S(1)} collective-permute-done((f32[16,128]{1,0:T(8,128)S(1)}, f32[16,128]{1,0:T(8,128)S(1)}, u32[]{:S(2)}, u32[]{:S(2)}) %collective-permute-start.11) | collective-permute-done | bytes 8224 | tf_op jit(solution)/shard_map/ppermute | solution.py:22
  96.1 3.0 %collective-permute-done.12 = f32[16,128]{1,0:T(8,128)S(1)} collective-permute-done((f32[16,128]{1,0:T(8,128)S(1)}, f32[16,128]{1,0:T(8,128)S(1)}, u32[]{:S(2)}, u32[]{:S(2)}) %collective-permute-start.12) | collective-permute-done | bytes 8224 | tf_op jit(solution)/shard_map/ppermute | solution.py:22
  99.2 2.1 %collective-permute-start.13 = (f32[16,128]{1,0:T(8,128)S(1)}, f32[16,128]{1,0:T(8,128)S(1)}, u32[]{:S(2)}, u32[]{:S(2)}) collective-permute-start(f32[16,128]{1,0:T(8,128)S(1)} %max.35), channel_id=1, source_target_pairs={{0,128},{1,129},{2,130},{3,131},{4,132},{5,133},{6,134},{7,135},{8... | collective-permute-start | bytes 24584 | tf_op jit(solution)/shard_map/ppermute | solution.py:22
  101.3 1.4 collective-permute-done.13
  102.7 4.5 %collective-permute-start.14 = (f32[16,128]{1,0:T(8,128)S(1)}, f32[16,128]{1,0:T(8,128)S(1)}, u32[]{:S(2)}, u32[]{:S(2)}) collective-permute-start(f32[16,128]{1,0:T(8,128)S(1)} %max.36), channel_id=1, source_target_pairs={{0,1},{1,0},{2,3},{3,2},{4,5},{5,4},{6,7},{7,6},{8,9},{9,8},{10,11... | collective-permute-start | bytes 24584 | tf_op jit(solution)/shard_map/ppermute | solution.py:22
  107.8 1.4 collective-permute-done.14
  111.8 1.6 pad_maximum_fusion.1
  113.4 6.8 %all-gather.2.cloned.1.call-done.g_ref = bf16[2048,3328]{1,0:T(8,128)(2,1)} async-done(((bf16[64,3328]{1,0:T(8,128)(2,1)}), bf16[2048,3328]{1,0:T(8,128)(2,1)}) %all-gather.2.cloned.1.call-update) | async-done | bytes 13631504 | tf_op jit(solution)/shard_map/all_gather | solution.py:109
  120.2 9.0 %shard_map.51 = f32[1024,512]{1,0:T(8,128)} custom-call(s32[2]{0:T(128)} %get-tuple-element.49.order_ref, bf16[2048,3328]{1,0:T(8,128)(2,1)} %all-gather.2.cloned.1.call-done.g_ref, bf16[512,3328]{1,0:T(8,128)(2,1)} %w_ref.3), custom_call_target="tpu_custom_call" | custom-call | tf_op jit(solution)/shard_map/pallas_call | solution.py:83
  132.2 2.7 %collective-permute-start.15 = (f16[2,2,128,512]{3,2,1,0:T(8,128)(2,1)S(1)}, f16[2,2,128,512]{3,2,1,0:T(8,128)(2,1)S(1)}, u32[]{:S(2)}, u32[]{:S(2)}) collective-permute-start(f16[2,2,128,512]{3,2,1,0:T(8,128)(2,1)S(1)} %fusion.3), channel_id=1, source_target_pairs={{0,2},{1,3},{2,0},{3,1},{4,6},{5,7},{6,4},{7,5},{8,14},{9,15},{10,... | collective-permute-start | bytes 1572872 | tf_op jit(solution)/shard_map/ppermute | solution.py:22
  134.9 9.0 %shard_map.50 = f32[1024,512]{1,0:T(8,128)} custom-call(s32[2]{0:T(128)} %get-tuple-element.48.order_ref, bf16[2048,3328]{1,0:T(8,128)(2,1)} %all-gather.2.cloned.1.call-done.g_ref, bf16[512,3328]{1,0:T(8,128)(2,1)} %w_ref.3), custom_call_target="tpu_custom_call" | custom-call | tf_op jit(solution)/shard_map/pallas_call | solution.py:83
  144.0 3.1 %collective-permute-done.15 = f16[2,2,128,512]{3,2,1,0:T(8,128)(2,1)S(1)} collective-permute-done((f16[2,2,128,512]{3,2,1,0:T(8,128)(2,1)S(1)}, f16[2,2,128,512]{3,2,1,0:T(8,128)(2,1)S(1)}, u32[]{:S(2)}, u32[]{:S(2)}) %collective-permute-start.15) | collective-permute-done | bytes 524320 | tf_op jit(solution)/shard_map/ppermute | solution.py:22
  147.1 1.9 bitcast_add_fusion
  149.3 1.5 collective-permute-start.21
  150.8 3.9 %collective-permute-done.16 = f16[2,128,512]{2,1,0:T(8,128)(2,1)S(1)} collective-permute-done((f16[2,128,512]{2,1,0:T(8,128)(2,1)S(1)}, f16[2,128,512]{2,1,0:T(8,128)(2,1)S(1)}, u32[]{:S(2)}, u32[]{:S(2)}) %collective-permute-start.16) | collective-permute-done | bytes 262176 | tf_op jit(solution)/shard_map/ppermute | solution.py:22
  154.8 4.1 %collective-permute-start.17 = (f16[128,512]{1,0:T(8,128)(2,1)S(1)}, f16[128,512]{1,0:T(8,128)(2,1)S(1)}, u32[]{:S(2)}, u32[]{:S(2)}) collective-permute-start(f16[128,512]{1,0:T(8,128)(2,1)S(1)} %fusion.14), channel_id=1, source_target_pairs={{0,1},{1,0},{2,3},{3,2},{4,5},{5,4},{6,7},{7,6},{8,9},{9,8},{10,11... | collective-permute-start | bytes 393224 | tf_op jit(solution)/shard_map/ppermute | solution.py:22
  159.0 2.7 %collective-permute-start.22 = (f16[128,512]{1,0:T(8,128)(2,1)S(1)}, f16[128,512]{1,0:T(8,128)(2,1)S(1)}, u32[]{:S(2)}, u32[]{:S(2)}) collective-permute-start(f16[128,512]{1,0:T(8,128)(2,1)S(1)} %fusion.15), channel_id=1, source_target_pairs={{0,1},{1,0},{2,3},{3,2},{4,5},{5,4},{6,7},{7,6},{8,9},{9,8},{10,11... | collective-permute-start | bytes 393224 | tf_op jit(solution)/shard_map/ppermute | solution.py:22
  162.8 8.2 %collective-permute-start.18 = (bf16[64,512]{1,0:T(8,128)(2,1)S(1)}, bf16[64,512]{1,0:T(8,128)(2,1)S(1)}, u32[]{:S(2)}, u32[]{:S(2)}) collective-permute-start(bf16[64,512]{1,0:T(8,128)(2,1)S(1)} %get-tuple-element.45), channel_id=1, source_target_pairs={{0,8},{1,9},{2,10},{3,11},{4,12},{5,13},{6,14},{7,15},{8,0},{9,1},... | collective-permute-start | bytes 196616 | tf_op jit(solution)/shard_map/ppermute | solution.py:22
  171.5 1.7 collective-permute-start.23
  173.2 6.9 %collective-permute-start.19 = (bf16[2,64,512]{2,1,0:T(8,128)(2,1)S(1)}, bf16[2,64,512]{2,1,0:T(8,128)(2,1)S(1)}, u32[]{:S(2)}, u32[]{:S(2)}) collective-permute-start(bf16[2,64,512]{2,1,0:T(8,128)(2,1)S(1)} %maximum_select_fusion.1), channel_id=1, source_target_pairs={{0,0},{1,32},{2,64},{3,96},{4,128},{5,160},{6,192},{7,224},{8,8},{... | collective-permute-start | bytes 393224 | tf_op jit(solution)/shard_map/ppermute | solution.py:22
  180.2 3.3 %collective-permute-start.24 = (bf16[2,64,512]{2,1,0:T(8,128)(2,1)S(1)}, bf16[2,64,512]{2,1,0:T(8,128)(2,1)S(1)}, u32[]{:S(2)}, u32[]{:S(2)}) collective-permute-start(bf16[2,64,512]{2,1,0:T(8,128)(2,1)S(1)} %maximum_select_fusion.2), channel_id=1, source_target_pairs={{0,16},{1,48},{2,80},{3,112},{4,144},{5,176},{6,208},{7,240},{8,24... | collective-permute-start | bytes 393224 | tf_op jit(solution)/shard_map/ppermute | solution.py:22
  183.5 12.8 %convolution_multiply_fusion = f32[512,3328]{1,0:T(8,128)} fusion(bf16[2048,512]{1,0:T(8,128)(2,1)S(1)} %bitcast.109, bf16[2048,3328]{1,0:T(8,128)(2,1)} %all-gather.2.cloned.1.call-done.g_ref), kind=kOutput, calls=%fused_computation | convolution fusion | flops 6981025792 | bytes 22544384 | tf_op jit(solution)/shard_map/dot_general | solution.py:155
  (80 shorter events, 17.1 us)
Async XLA Ops:
  7.2 113.1 %all-gather.2.cloned.1.call-start = ((), (), s32[]{:S(2)}) async-start(), calls=%async_computation | async-start | bytes 14057472 | tf_op jit(solution)/shard_map/all_gather | solution.py:109
  9.7 4.6 %copy-start.1 = (bf16[64,3328]{1,0:T(8,128)(2,1)S(1)}, bf16[64,3328]{1,0:T(8,128)(2,1)}, u32[]{:S(2)}) copy-start(bf16[64,3328]{1,0:T(8,128)(2,1)} %param.4) | copy-start | bytes 1277956
  9.7 3.8 %collective-permute-start = (bf16[2,64,512]{2,1,0:T(8,128)(2,1)S(1)}, bf16[2,64,512]{2,1,0:T(8,128)(2,1)S(1)}, u32[]{:S(2)}, u32[]{:S(2)}) collective-permute-start(bf16[2,64,512]{2,1,0:T(8,128)(2,1)S(1)} %pad_maximum_fusion.6), channel_id=1, source_target_pairs={{0,8},{1,9},{2,10},{3,11},{4,12},{5,13},{6,14},{7,15},{8,0},{9,1},... | collective-permute-start | bytes 393224 | tf_op jit(solution)/shard_map/ppermute | solution.py:22
  13.6 4.6 %collective-permute-start.1 = (bf16[2,2,64,512]{3,2,0,1:T(8,128)(2,1)S(1)}, bf16[2,2,64,512]{3,2,0,1:T(8,128)(2,1)S(1)}, u32[]{:S(2)}, u32[]{:S(2)}) collective-permute-start(bf16[2,2,64,512]{3,2,0,1:T(8,128)(2,1)S(1)} %maximum_select_fusion), channel_id=1, source_target_pairs={{0,0},{1,1},{2,2},{3,3},{4,4},{5,5},{6,6},{7,7},{8,8},{9,9},{10,10... | collective-permute-start | bytes 786440 | tf_op jit(solution)/shard_map/ppermute | solution.py:22
  16.3 1.2 collective-permute-start.4
  17.6 10.7 %collective-permute-start.5 = (f32[16,128]{1,0:T(8,128)S(1)}, f32[16,128]{1,0:T(8,128)S(1)}, u32[]{:S(2)}, u32[]{:S(2)}) collective-permute-start(f32[16,128]{1,0:T(8,128)S(1)} %broadcast_maximum_fusion), channel_id=1, source_target_pairs={{0,16},{1,17},{2,18},{3,19},{4,20},{5,21},{6,22},{7,23},{8,24},{9,... | collective-permute-start | bytes 24584 | tf_op jit(solution)/shard_map/ppermute | solution.py:22
  18.1 17.4 %collective-permute-start.2 = (bf16[2,64,512]{2,1,0:T(8,128)(2,1)S(1)}, bf16[2,64,512]{2,1,0:T(8,128)(2,1)S(1)}, u32[]{:S(2)}, u32[]{:S(2)}) collective-permute-start(bf16[2,64,512]{2,1,0:T(8,128)(2,1)S(1)} %get-tuple-element.33), channel_id=1, source_target_pairs={{0,0},{1,32},{2,66},{3,98},{4,132},{5,164},{6,198},{7,230},{8,8},{... | collective-permute-start | bytes 393224 | tf_op jit(solution)/shard_map/ppermute | solution.py:22
  27.5 14.0 %collective-permute-start.3 = (bf16[2,64,512]{2,1,0:T(8,128)(2,1)S(1)}, bf16[2,64,512]{2,1,0:T(8,128)(2,1)S(1)}, u32[]{:S(2)}, u32[]{:S(2)}) collective-permute-start(bf16[2,64,512]{2,1,0:T(8,128)(2,1)S(1)} %get-tuple-element.32), channel_id=1, source_target_pairs={{0,16},{1,48},{2,82},{3,114},{4,148},{5,180},{6,214},{7,246},{8,24... | collective-permute-start | bytes 393224 | tf_op jit(solution)/shard_map/ppermute | solution.py:22
  28.3 7.2 %collective-permute-start.6 = (f32[16,128]{1,0:T(8,128)S(1)}, f32[16,128]{1,0:T(8,128)S(1)}, u32[]{:S(2)}, u32[]{:S(2)}) collective-permute-start(f32[16,128]{1,0:T(8,128)S(1)} %fusion.25), channel_id=1, source_target_pairs={{0,2},{1,3},{2,0},{3,1},{4,6},{5,7},{6,4},{7,5},{8,10},{9,11},{10,... | collective-permute-start | bytes 24584 | tf_op jit(solution)/shard_map/ppermute | solution.py:22
  41.7 20.7 %collective-permute-start.7 = (bf16[2,2,64,512]{3,2,1,0:T(8,128)(2,1)S(1)}, bf16[2,2,64,512]{3,2,1,0:T(8,128)(2,1)S(1)}, u32[]{:S(2)}, u32[]{:S(2)}) collective-permute-start(bf16[2,2,64,512]{3,2,1,0:T(8,128)(2,1)S(1)} %get-tuple-element.28), channel_id=1, source_target_pairs={{0,1},{1,0},{2,3},{3,2},{4,5},{5,4},{6,7},{7,6},{8,9},{9,8},{10,11... | collective-permute-start | bytes 786440 | tf_op jit(solution)/shard_map/ppermute | solution.py:22
  62.6 17.0 %collective-permute-start.8 = (bf16[2,2,2,64,512]{4,3,2,1,0:T(8,128)(2,1)S(1)}, bf16[2,2,2,64,512]{4,3,2,1,0:T(8,128)(2,1)S(1)}, u32[]{:S(2)}, u32[]{:S(2)}) collective-permute-start(bf16[2,2,2,64,512]{4,3,2,1,0:T(8,128)(2,1)S(1)} %get-tuple-element.23), channel_id=1, source_target_pairs={{0,2},{1,3},{2,0},{3,1},{4,6},{5,7},{6,4},{7,5},{8,14},{9,15},{10,... | collective-permute-start | bytes 1572872 | tf_op jit(solution)/shard_map/ppermute | solution.py:22
  79.7 31.5 %collective-permute-start.9 = (bf16[2,2,2,2,64,512]{5,4,3,2,1,0:T(8,128)(2,1)S(1)}, bf16[2,2,2,2,64,512]{5,4,3,2,1,0:T(8,128)(2,1)S(1)}, u32[]{:S(2)}, u32[]{:S(2)}) collective-permute-start(bf16[2,2,2,2,64,512]{5,4,3,2,1,0:T(8,128)(2,1)S(1)} %pad_maximum_fusion.2), channel_id=1, source_target_pairs={{0,6},{1,7},{2,4},{3,5},{4,2},{5,3},{6,0},{7,1},{8,10},{9,11},{10,... | collective-permute-start | bytes 3145736 | tf_op jit(solution)/shard_map/ppermute | solution.py:22
  79.9 4.0 %collective-permute-start.10 = (f32[16,128]{1,0:T(8,128)S(1)}, f32[16,128]{1,0:T(8,128)S(1)}, u32[]{:S(2)}, u32[]{:S(2)}) collective-permute-start(f32[16,128]{1,0:T(8,128)S(1)} %max.32), channel_id=1, source_target_pairs={{0,32},{1,33},{2,34},{3,35},{4,36},{5,37},{6,38},{7,39},{8,40},{9,... | collective-permute-start | bytes 24584 | tf_op jit(solution)/shard_map/ppermute | solution.py:22
  83.9 12.2 %collective-permute-start.11 = (f32[16,128]{1,0:T(8,128)S(1)}, f32[16,128]{1,0:T(8,128)S(1)}, u32[]{:S(2)}, u32[]{:S(2)}) collective-permute-start(f32[16,128]{1,0:T(8,128)S(1)} %max.33), channel_id=1, source_target_pairs={{0,4},{1,5},{2,6},{3,7},{4,0},{5,1},{6,2},{7,3},{8,12},{9,13},{10,... | collective-permute-start | bytes 24584 | tf_op jit(solution)/shard_map/ppermute | solution.py:22
  96.1 3.0 %collective-permute-start.12 = (f32[16,128]{1,0:T(8,128)S(1)}, f32[16,128]{1,0:T(8,128)S(1)}, u32[]{:S(2)}, u32[]{:S(2)}) collective-permute-start(f32[16,128]{1,0:T(8,128)S(1)} %max.34), channel_id=1, source_target_pairs={{0,64},{1,65},{2,66},{3,67},{4,68},{5,69},{6,70},{7,71},{8,72},{9,... | collective-permute-start | bytes 24584 | tf_op jit(solution)/shard_map/ppermute | solution.py:22
  99.2 3.5 %collective-permute-start.13 = (f32[16,128]{1,0:T(8,128)S(1)}, f32[16,128]{1,0:T(8,128)S(1)}, u32[]{:S(2)}, u32[]{:S(2)}) collective-permute-start(f32[16,128]{1,0:T(8,128)S(1)} %max.35), channel_id=1, source_target_pairs={{0,128},{1,129},{2,130},{3,131},{4,132},{5,133},{6,134},{7,135},{8... | collective-permute-start | bytes 24584 | tf_op jit(solution)/shard_map/ppermute | solution.py:22
  102.7 6.6 %collective-permute-start.14 = (f32[16,128]{1,0:T(8,128)S(1)}, f32[16,128]{1,0:T(8,128)S(1)}, u32[]{:S(2)}, u32[]{:S(2)}) collective-permute-start(f32[16,128]{1,0:T(8,128)S(1)} %max.36), channel_id=1, source_target_pairs={{0,1},{1,0},{2,3},{3,2},{4,5},{5,4},{6,7},{7,6},{8,9},{9,8},{10,11... | collective-permute-start | bytes 24584 | tf_op jit(solution)/shard_map/ppermute | solution.py:22
  131.9 12.0 %collective-permute-start.20 = (f16[2,2,128,512]{3,2,1,0:T(8,128)(2,1)S(1)}, f16[2,2,128,512]{3,2,1,0:T(8,128)(2,1)S(1)}, u32[]{:S(2)}, u32[]{:S(2)}) collective-permute-start(f16[2,2,128,512]{3,2,1,0:T(8,128)(2,1)S(1)} %fusion.2), channel_id=1, source_target_pairs={{0,2},{1,3},{2,0},{3,1},{4,6},{5,7},{6,4},{7,5},{8,14},{9,15},{10,... | collective-permute-start | bytes 1572872 | tf_op jit(solution)/shard_map/ppermute | solution.py:22
  132.2 14.8 %collective-permute-start.15 = (f16[2,2,128,512]{3,2,1,0:T(8,128)(2,1)S(1)}, f16[2,2,128,512]{3,2,1,0:T(8,128)(2,1)S(1)}, u32[]{:S(2)}, u32[]{:S(2)}) collective-permute-start(f16[2,2,128,512]{3,2,1,0:T(8,128)(2,1)S(1)} %fusion.3), channel_id=1, source_target_pairs={{0,2},{1,3},{2,0},{3,1},{4,6},{5,7},{6,4},{7,5},{8,14},{9,15},{10,... | collective-permute-start | bytes 1572872 | tf_op jit(solution)/shard_map/ppermute | solution.py:22
  149.1 5.6 %collective-permute-start.16 = (f16[2,128,512]{2,1,0:T(8,128)(2,1)S(1)}, f16[2,128,512]{2,1,0:T(8,128)(2,1)S(1)}, u32[]{:S(2)}, u32[]{:S(2)}) collective-permute-start(f16[2,128,512]{2,1,0:T(8,128)(2,1)S(1)} %fusion.8), channel_id=1, source_target_pairs={{0,6},{1,7},{2,4},{3,5},{4,2},{5,3},{6,0},{7,1},{8,10},{9,11},{10,... | collective-permute-start | bytes 786440 | tf_op jit(solution)/shard_map/ppermute | solution.py:22
  149.3 9.6 %collective-permute-start.21 = (f16[2,128,512]{2,1,0:T(8,128)(2,1)S(1)}, f16[2,128,512]{2,1,0:T(8,128)(2,1)S(1)}, u32[]{:S(2)}, u32[]{:S(2)}) collective-permute-start(f16[2,128,512]{2,1,0:T(8,128)(2,1)S(1)} %fusion.9), channel_id=1, source_target_pairs={{0,6},{1,7},{2,4},{3,5},{4,2},{5,3},{6,0},{7,1},{8,10},{9,11},{10,... | collective-permute-start | bytes 786440 | tf_op jit(solution)/shard_map/ppermute | solution.py:22
  154.8 28.7 %copy-start = (bf16[4,2,2,2,64,512]{5,4,3,2,1,0:T(8,128)(2,1)S(1)}, bf16[4,2,2,2,64,512]{5,4,3,2,1,0:T(8,128)(2,1)}, u32[]{:S(2)}) copy-start(bf16[4,2,2,2,64,512]{5,4,3,2,1,0:T(8,128)(2,1)} %pad_maximum_fusion.1) | copy-start | bytes 6291460
  154.8 7.9 %collective-permute-start.17 = (f16[128,512]{1,0:T(8,128)(2,1)S(1)}, f16[128,512]{1,0:T(8,128)(2,1)S(1)}, u32[]{:S(2)}, u32[]{:S(2)}) collective-permute-start(f16[128,512]{1,0:T(8,128)(2,1)S(1)} %fusion.14), channel_id=1, source_target_pairs={{0,1},{1,0},{2,3},{3,2},{4,5},{5,4},{6,7},{7,6},{8,9},{9,8},{10,11... | collective-permute-start | bytes 393224 | tf_op jit(solution)/shard_map/ppermute | solution.py:22
  159.0 12.4 %collective-permute-start.22 = (f16[128,512]{1,0:T(8,128)(2,1)S(1)}, f16[128,512]{1,0:T(8,128)(2,1)S(1)}, u32[]{:S(2)}, u32[]{:S(2)}) collective-permute-start(f16[128,512]{1,0:T(8,128)(2,1)S(1)} %fusion.15), channel_id=1, source_target_pairs={{0,1},{1,0},{2,3},{3,2},{4,5},{5,4},{6,7},{7,6},{8,9},{9,8},{10,11... | collective-permute-start | bytes 393224 | tf_op jit(solution)/shard_map/ppermute | solution.py:22
  162.8 10.4 %collective-permute-start.18 = (bf16[64,512]{1,0:T(8,128)(2,1)S(1)}, bf16[64,512]{1,0:T(8,128)(2,1)S(1)}, u32[]{:S(2)}, u32[]{:S(2)}) collective-permute-start(bf16[64,512]{1,0:T(8,128)(2,1)S(1)} %get-tuple-element.45), channel_id=1, source_target_pairs={{0,8},{1,9},{2,10},{3,11},{4,12},{5,13},{6,14},{7,15},{8,0},{9,1},... | collective-permute-start | bytes 196616 | tf_op jit(solution)/shard_map/ppermute | solution.py:22
  171.5 8.7 %collective-permute-start.23 = (bf16[64,512]{1,0:T(8,128)(2,1)S(1)}, bf16[64,512]{1,0:T(8,128)(2,1)S(1)}, u32[]{:S(2)}, u32[]{:S(2)}) collective-permute-start(bf16[64,512]{1,0:T(8,128)(2,1)S(1)} %get-tuple-element.43), channel_id=1, source_target_pairs={{0,8},{1,9},{2,10},{3,11},{4,12},{5,13},{6,14},{7,15},{8,0},{9,1},... | collective-permute-start | bytes 196616 | tf_op jit(solution)/shard_map/ppermute | solution.py:22
  173.2 23.0 %collective-permute-start.19 = (bf16[2,64,512]{2,1,0:T(8,128)(2,1)S(1)}, bf16[2,64,512]{2,1,0:T(8,128)(2,1)S(1)}, u32[]{:S(2)}, u32[]{:S(2)}) collective-permute-start(bf16[2,64,512]{2,1,0:T(8,128)(2,1)S(1)} %maximum_select_fusion.1), channel_id=1, source_target_pairs={{0,0},{1,32},{2,64},{3,96},{4,128},{5,160},{6,192},{7,224},{8,8},{... | collective-permute-start | bytes 393224 | tf_op jit(solution)/shard_map/ppermute | solution.py:22
  180.2 16.1 %collective-permute-start.24 = (bf16[2,64,512]{2,1,0:T(8,128)(2,1)S(1)}, bf16[2,64,512]{2,1,0:T(8,128)(2,1)S(1)}, u32[]{:S(2)}, u32[]{:S(2)}) collective-permute-start(bf16[2,64,512]{2,1,0:T(8,128)(2,1)S(1)} %maximum_select_fusion.2), channel_id=1, source_target_pairs={{0,16},{1,48},{2,80},{3,112},{4,144},{5,176},{6,208},{7,240},{8,24... | collective-permute-start | bytes 393224 | tf_op jit(solution)/shard_map/ppermute | solution.py:22
Sparse Core Ops, SparseCore 0:
  9.9 110.3 all-gather.1
